TPU v7x, 512 devices: a whole 4x8x8 slice. The times are simulated.
512 devices in a mesh: rep: 8 (over y_lo, core), shard: 64 (over y_hi, z, x).
Axes of the slice: x: 4, y: 8 (y_hi: 2, y_lo: 4; y = y_hi * 4 + y_lo), z: 8, core: 2. Of those that a mesh axis runs over, the one named last changes fastest.
Arguments:
- grad_parts: bfloat16 [8, 64, 576, 1152], P('rep', 'shard'), may hold values from -64 to 64
- master: float32 [576, 1152], P('shard'), may hold values from -0.06 to 0.06
- moment_one: float32 [576, 1152], P('shard'), may hold values from -0.12 to 0.12
- moment_two: float32 [576, 1152], P('shard'), may hold values from 0.0001 to 0.01
- step_count: int32 [1], replicated, may hold values from 1 to 20
Outputs:
- new_master: float32 [576, 1152], P('shard')
- new_moment_one: float32 [576, 1152], P('shard')
- new_moment_two: float32 [576, 1152], P('shard')
- adam_direction: float32 [576, 1152], P('shard')
- params: bfloat16 [576, 1152], replicated
All inputs are finite; a program needn't handle non-finite values.
Results may differ from a plain program's by a relative error of at most 0.024.
Values may be sent and summed in bfloat16 or wider, within the bound.
A program may use at most 64 MiB of HBM per device.

v0:
```python
import jax
import jax.numpy as jnp
from jax import lax
from jax.sharding import PartitionSpec as P

BETA_ONE = 0.9
BETA_TWO = 0.95
LEARN_RATE = 0.001
EPSILON = 1e-08


def adam_step(gradient, master, moment_one, moment_two, step_count):
    new_moment_one = BETA_ONE * moment_one + (1.0 - BETA_ONE) * gradient
    new_moment_two = BETA_TWO * moment_two + (1.0 - BETA_TWO) * gradient * gradient
    steps_float = step_count[0].astype(jnp.float32)
    first_fix = 1.0 - jnp.power(jnp.float32(BETA_ONE), steps_float)
    second_fix = 1.0 - jnp.power(jnp.float32(BETA_TWO), steps_float)
    direction = new_moment_one / first_fix / (jnp.sqrt(new_moment_two / second_fix) + EPSILON)
    new_master = master - LEARN_RATE * direction
    return (new_master, new_moment_one, new_moment_two, direction)


def local(grad_parts, master, moment_one, moment_two, step_count):
    partial_value = grad_parts.reshape(grad_parts.shape[2], grad_parts.shape[3]).astype(jnp.float32)
    devices_total = lax.axis_size("rep") * lax.axis_size("shard")
    row_block = lax.psum_scatter(partial_value, "shard", scatter_dimension=0, tiled=True)
    summed = lax.psum(row_block, "rep")
    results = adam_step(summed / devices_total, master, moment_one, moment_two, step_count)
    new_master, new_moment_one, new_moment_two, direction = results
    params = lax.all_gather(new_master.astype(jnp.bfloat16), "shard", axis=0, tiled=True)
    return (new_master, new_moment_one, new_moment_two, direction, params)


def solution(mesh):
    placed = (
        P("rep", "shard", None, None),
        P("shard", None),
        P("shard", None),
        P("shard", None),
        P(),
    )
    return jax.shard_map(
        local,
        mesh=mesh,
        in_specs=placed,
        out_specs=(P("shard", None), P("shard", None), P("shard", None), P("shard", None), P()),
        check_vma=False,
    )
```

profile of v0, /device:TPU:1, one launch (start us, length us, event | category | flops | bytes accessed | tf_op | source)
XLA Modules:
  0.0 1017.2 jit_solution(6413098635314897203)
XLA Ops:
  7.2 0.0 copy-start
  7.2 0.0 copy-start.2
  7.2 0.0 copy-start.1
  7.2 0.0 all-reduce.3.cloned.1.call-start
  7.2 3.1 bitcast_convert_fusion
  10.3 0.0 all-reduce.3.cloned.1.call-update
  10.3 0.0 all-gather.3.cloned.1.call-start
  11.1 1.3 dynamic-slice
  13.0 797.3 %all-reduce.3.cloned.1.call-done = f32[576,1152]{1,0:T(8,128)} async-done(((f32[576,1152]{1,0:T(8,128)}), f32[576,1152]{1,0:T(8,128)}) %all-reduce.3.cloned.1.call-update) | async-done | bytes 2654224
  810.3 0.9 constant_dynamic-slice_fusion
  811.2 64.1 %psum.7 = f32[9,1152]{1,0:T(8,128)S(1)} all-reduce(f32[9,1152]{1,0:T(8,128)S(1)} %constant_dynamic-slice_fusion), channel_id=1, replica_groups=mesh['rep'=8,'shard'=64] {'rep'}, use_global_device_ids=true, to_apply=%region_1.0 | all-reduce | flops 10368 | bytes 82944 | tf_op jit(solution)/shard_map/psum | solution.py:27
  875.3 0.0 copy-done
  875.3 0.0 copy-done.2
  875.3 0.0 copy-done.1
  875.3 0.7 convert_bitcast_fusion
  876.0 0.0 all-gather.3.cloned.1.call-update
  876.1 130.6 %all-gather.3.cloned.1.call-done = bf16[64,9,1152]{2,1,0:T(8,128)(2,1)} async-done(((bf16[1,9,1152]{2,1,0:T(8,128)(2,1)}), bf16[64,9,1152]{2,1,0:T(8,128)(2,1)}) %all-gather.3.cloned.1.call-update) | async-done | bytes 1327120 | tf_op jit(solution)/shard_map/all_gather | solution.py:30
  1006.6 3.7 reshape.24
Async XLA Ops:
  7.2 868.1 %copy-start = (f32[9,1152]{1,0:T(8,128)S(1)}, f32[9,1152]{1,0:T(8,128)}, u32[]{:S(2)}) copy-start(f32[9,1152]{1,0:T(8,128)} %param.6) | copy-start | bytes 124420
  7.2 868.1 %copy-start.2 = (f32[9,1152]{1,0:T(8,128)S(1)}, f32[9,1152]{1,0:T(8,128)}, u32[]{:S(2)}) copy-start(f32[9,1152]{1,0:T(8,128)} %param.7) | copy-start | bytes 124420
  7.2 868.1 %copy-start.1 = (f32[9,1152]{1,0:T(8,128)S(1)}, f32[9,1152]{1,0:T(8,128)}, u32[]{:S(2)}) copy-start(f32[9,1152]{1,0:T(8,128)} %param.8) | copy-start | bytes 124420
  7.2 803.1 %all-reduce.3.cloned.1.call-start = ((), (), s32[]{:S(2)}) async-start(), calls=%async_computation.1 | async-start | bytes 5308416
  10.3 996.3 %all-gather.3.cloned.1.call-start = ((), (), s32[]{:S(2)}) async-start(), calls=%async_computation | async-start | bytes 2396160 | tf_op jit(solution)/shard_map/all_gather | solution.py:30
Sparse Core Ops, SparseCore 0:
  11.0 799.2 all-reduce.2
  876.2 130.3 all-gather.2
where the time goes:
time: 1020 us
  waiting for transfers between devices  928 us (91%)
  blocking collectives  64.1 us (6%)
  between operations  15.5 us (2%)
    unnamed x3, waiting for transfers between devices  797 us
    all_gather x1, waiting for transfers between devices, local(): lax.all_gather(new_master.astype(jnp.bfloat16), 'shard', axis=0, tiled=True)  131 us
    psum x1, blocking collectives, local(): summed = lax.psum(row_block, 'rep')  64.1 us
  transfers between devices with their start and end apart: 2, of which 2 were waited for; matrix products, arithmetic and copies ran while one was open for 0% of the time, Pallas kernels for 0%

commit v1 on v0

v1 whole, which is shorter than its diff:
```python
import math

import jax
import jax.numpy as jnp
from jax import lax
from jax.experimental import pallas as pl
from jax.experimental.pallas import tpu as pltpu
from jax.sharding import PartitionSpec as P

MESH = pl.DeviceIdType.MESH
F32, BF16 = jnp.float32, jnp.bfloat16
BETA_ONE = 0.9
BETA_TWO = 0.95
LEARN_RATE = 0.001
EPSILON = 1e-08

ROWS, D = 576, 1152
NA, NB = 6, 3
CA = NA * 128

LOC, S0, A1, B1, A2, B2, Y3, SIB, G1, GA2, GB2, GA3, GB3, FA, FB, END = (
    0, 4, 8, 12, 20, 28, 32, 40, 41, 42, 50, 54, 58, 66, 70, 74,
)


def kernel(
    grad, master, mom1, mom2, step,
    o_master, o_m1, o_m2, o_dir, o_par,
    own, sib, f, sa1, ra1, sb1, rb1, acc_a, acc_b, stage, sa2, ra2, sb2, rb2, s3, r3,
    gs, qs, pb2, gz, gx, ha, hb, o, send, recv,
):
    rep, shard = lax.axis_index("rep"), lax.axis_index("shard")
    c, y_lo = rep % 2, rep // 2
    x, z, y_hi = shard % 4, (shard // 4) % 8, shard // 32
    y = y_hi * 4 + y_lo
    z_lo = z % 4
    act = z // 4 == c

    def dev(x_, y_, z_, c_):
        return ((y_ % 4) * 2 + c_, (y_ // 4) * 32 + z_ * 4 + x_)

    def rdma(src, dst, ssem, rsem, where):
        return pltpu.make_async_remote_copy(
            src_ref=src, dst_ref=dst, send_sem=send.at[ssem], recv_sem=recv.at[rsem], device_id=where, device_id_type=MESH
        )

    sibling = dev(x, y, z, 1 - c)

    def wait_recv(ref, slot):
        rdma(ref, ref, slot, slot, sibling).wait_recv()

    def wait_send(ref, slot):
        rdma(ref, ref, slot, slot, sibling).wait_send()

    def own_copies(part):
        lo, n = ((CA, D - CA), (0, CA))[part]
        return [
            pltpu.make_async_copy(
                grad.at[pl.ds(pl.multiple_of(h * 288 + c * 144, 16), 144), pl.ds(lo, n)],
                own.at[h, :, pl.ds(lo, n)],
                recv.at[LOC + 2 * part + h],
            )
            for h in range(2)
        ]

    for part in range(2):
        for cp in own_copies(part):
            cp.start()

    barrier = pltpu.get_barrier_semaphore()

    def greet(where):
        pl.semaphore_signal(barrier, inc=1, device_id=where, device_id_type=MESH)

    greet(sibling)
    for d in range(1, 8):
        greet(dev(x, y, (z + d) % 8, c))
        greet(dev(x, (y + d) % 8, z, c))
    for d in range(1, 4):
        greet(dev((x + d) % 4, y, z, c))
    pl.semaphore_wait(barrier, 18)

    def sib_copies(part):
        lo, n = ((CA, D - CA), (0, CA))[part]
        return [
            rdma(
                grad.at[pl.ds(pl.multiple_of(h * 288 + (1 - c) * 144, 16), 144), pl.ds(lo, n)],
                sib.at[h, :, pl.ds(lo, n)],
                S0 + 2 * part + h, S0 + 2 * part + h, sibling,
            )
            for h in range(2)
        ]

    for part in range(2):
        for cp in sib_copies(part):
            cp.start()

    acc_a[pl.ds(432, 16), :] = jnp.zeros((16, 128), F32)
    acc_b[pl.ds(216, 40), :] = jnp.zeros((40, 128), F32)
    stage[pl.ds(216, 8), :] = jnp.zeros((8, 128), F32)

    def add_pair(part):
        for cp in own_copies(part):
            cp.wait()
        for cp in sib_copies(part):
            cp.wait_recv()
        for l in ((6, 7, 8), range(6))[part]:
            for h in range(2):
                cols = pl.ds(l * 128, 128)
                f[l, pl.ds(h * 144, 144), :] = own[h, :, cols].astype(F32) + sib[h, :, cols].astype(F32)

    add_pair(0)
    for j in range(4):
        for i in range(27):
            l, r = divmod(i, 9)
            for h in range(2):
                stage[pl.ds(i * 8 + h * 4, 4), :] = f[6 + l, pl.ds(h * 144 + j * 36 + r, 4, stride=9), :]
        sb1[j] = stage[...].astype(BF16)
        zt = 4 * c + j

        @pl.when(zt != z)
        def _():
            rdma(sb1.at[j], rb1.at[z], B1 + j, B1 + z, dev(x, y, zt, c)).start()

    add_pair(1)
    for d in (2, 1, 3, 0):
        xt = (x + d) % 4
        for t in range(27):
            pair = []
            for i in (2 * t, 2 * t + 1):
                l, r = divmod(i, 9)
                pair.append(f[l, pl.ds(9 * xt + r, 8, stride=36), :])
            sa1[xt, pl.ds(16 * t, 16), :] = jnp.concatenate(pair, 0).astype(BF16)
        if d:
            rdma(sa1.at[xt], ra1.at[x], A1 + xt, A1 + x, dev(xt, y, z, c)).start()

    @pl.when(act)
    def _():
        for d in range(1, 8):
            zs = (z + d) % 8
            wait_recv(rb1.at[zs], B1 + zs)
        total = sb1[z_lo].astype(F32)
        for d in range(1, 8):
            total += rb1[(z + d) % 8].astype(F32)
        acc_b[pl.ds(0, 224), :] = total
        for d in (2, 1, 3, 0):
            xt = (x + d) % 4
            rows = [acc_b[pl.ds(h * 4 + xt + 64 * i, 8, stride=8), :] for h in range(2) for i in range(4)]
            sb2[xt] = jnp.concatenate(rows, 0).astype(BF16)
            if d:
                rdma(sb2.at[xt], rb2.at[x], B2 + xt, B2 + x, dev(xt, y, z, c)).start()

    for d in range(1, 4):
        xs = (x + d) % 4
        wait_recv(ra1.at[xs], A1 + xs)
    total = sa1[x].astype(F32)
    for d in range(1, 4):
        total += ra1[(x + d) % 4].astype(F32)
    acc_a[pl.ds(0, 432), :] = total
    for j in range(4):
        zt = 4 * c + j
        rows = [acc_a[pl.ds(h * 4 + j + 64 * i, 8, stride=8), :] for h in range(2) for i in range(7)]
        sa2[j] = jnp.concatenate(rows, 0).astype(BF16)

        @pl.when(zt != z)
        def _():
            rdma(sa2.at[j], ra2.at[z], A2 + j, A2 + z, dev(x, y, zt, c)).start()

    @pl.when(act)
    def _():
        for d in range(1, 4):
            xs = (x + d) % 4
            wait_recv(rb2.at[xs], B2 + xs)
        tb = sb2[x].astype(F32)
        for d in range(1, 4):
            tb += rb2[(x + d) % 4].astype(F32)
        for d in range(1, 8):
            zs = (z + d) % 8
            wait_recv(ra2.at[zs], A2 + zs)
        ta = sa2[z_lo].astype(F32)
        for d in range(1, 8):
            ta += ra2[(z + d) % 8].astype(F32)
        for h in range(2):
            s3[h] = jnp.concatenate([ta[h * 56 : h * 56 + 56], tb[h * 32 : h * 32 + 32], jnp.zeros((8, 128), F32)], 0).astype(BF16)
        for d in (4, 3, 5, 2, 6, 1, 7):
            yt = (y + d) % 8
            rdma(s3.at[yt // 4], r3.at[y], Y3 + yt, Y3 + y, dev(x, yt, z, c)).start()
        for d in range(1, 8):
            ys = (y + d) % 8
            wait_recv(r3.at[ys], Y3 + ys)
        g = s3[y_hi].astype(F32)
        for d in range(1, 8):
            g += r3[(y + d) % 8].astype(F32)
        gs[...] = g
        rdma(gs, gs, SIB, SIB, sibling).start()

    @pl.when(jnp.logical_not(act))
    def _():
        wait_recv(gs, SIB)

    steps = jnp.full((9, 128), step[0], jnp.int32).astype(F32)
    first_fix = 1.0 - jnp.exp(steps * math.log(BETA_ONE))
    second_fix = 1.0 - jnp.exp(steps * math.log(BETA_TWO))
    for l in range(9):
        q = l * 9 + (2 if l >= 6 else 0)
        cols = pl.ds(l * 128, 128)
        g = gs[pl.ds(q, 9), :] * (1.0 / 512.0)
        n1 = BETA_ONE * mom1[:, cols] + (1.0 - BETA_ONE) * g
        n2 = BETA_TWO * mom2[:, cols] + (1.0 - BETA_TWO) * g * g
        direction = n1 / first_fix / (jnp.sqrt(n2 / second_fix) + EPSILON)
        nm = master[:, cols] - LEARN_RATE * direction
        o_m1[:, cols] = n1
        o_m2[:, cols] = n2
        o_dir[:, cols] = direction
        o_master[:, cols] = nm
        qs[pl.ds(q, 9), :] = nm

    @pl.when(act)
    def _():
        qs[pl.ds(54, 2), :] = jnp.zeros((2, 128), F32)
        qs[pl.ds(83, 13), :] = jnp.zeros((13, 128), F32)
        pb2[y_hi] = qs[...].astype(BF16)
        rdma(pb2.at[y_hi], pb2.at[y_hi], G1, G1, dev(x, 7 - y, z, c)).start()
        wait_recv(pb2.at[1 - y_hi], G1)
        both = [pb2[h].astype(F32) for h in range(2)]
        gz[z_lo] = jnp.concatenate([b[0:56] for b in both], 0).astype(BF16)
        gx[x] = jnp.concatenate([b[56:88] for b in both], 0).astype(BF16)
        for d in (2, 1, 3):
            xt = (x + d) % 4
            rdma(gx.at[x], gx.at[x], GB2 + xt, GB2 + x, dev(xt, y, z, c)).start()
        for d in (4, 3, 5, 2, 6, 1, 7):
            zt = (z + d) % 8
            rdma(gz.at[z_lo], gz.at[z_lo], GA2 + zt, GA2 + z_lo, dev(x, y, zt, c)).start()
        for d in range(1, 4):
            xs = (x + d) % 4
            wait_recv(gx.at[xs], GB2 + xs)
        for xs in range(4):
            v = gx[xs].astype(F32)
            for h in range(2):
                for i in range(4):
                    acc_b[pl.ds(h * 4 + xs + 64 * i, 8, stride=8), :] = v[h * 32 + i * 8 : h * 32 + i * 8 + 8]
        hb[c, z_lo] = acc_b[pl.ds(0, 224), :].astype(BF16)
        for d in (4, 3, 5, 2, 6, 1, 7):
            zt = (z + d) % 8
            rdma(hb.at[c, z_lo], hb.at[c, z_lo], GB3 + zt, GB3 + z_lo, dev(x, y, zt, c)).start()

    for j in range(4):
        @pl.when(4 * c + j != z)
        def _():
            wait_recv(gz.at[j], GA2 + j)

    for j in range(4):
        v = gz[j].astype(F32)
        for h in range(2):
            for i in range(7):
                acc_a[pl.ds(h * 4 + j + 64 * i, 8, stride=8), :] = v[h * 56 + i * 8 : h * 56 + i * 8 + 8]
    ha[c, x] = acc_a[pl.ds(0, 432), :].astype(BF16)
    for d in (2, 1, 3):
        xt = (x + d) % 4
        rdma(ha.at[c, x], ha.at[c, x], GA3 + xt, GA3 + x, dev(xt, y, z, c)).start()

    def unpack_a(zh, xs):
        v = ha[zh, xs].astype(F32)
        for i in range(54):
            l, r = divmod(i, 9)
            o[zh, l, pl.ds(9 * xs + r, 8, stride=36), :] = v[8 * i : 8 * i + 8]

    def unpack_b(zh, j):
        v = hb[zh, j].astype(F32)
        for i in range(27):
            l, r = divmod(i, 9)
            for h in range(2):
                o[zh, 6 + l, pl.ds(h * 144 + j * 36 + r, 4, stride=9), :] = v[8 * i + 4 * h : 8 * i + 4 * h + 4]

    def pass_on(ref, slot):
        rdma(ref, ref, slot, slot, sibling).start()

    pass_on(ha.at[c, x], FA + x)
    for d in (1, 3, 2):
        xs = (x + d) % 4
        wait_recv(ha.at[c, xs], GA3 + xs)
        pass_on(ha.at[c, xs], FA + xs)
    for j in range(4):
        @pl.when(4 * c + j != z)
        def _():
            wait_recv(hb.at[c, j], GB3 + j)

        pass_on(hb.at[c, j], FB + j)
    for j in range(4):
        unpack_a(c, j)
        unpack_b(c, j)
    for j in range(4):
        wait_recv(ha.at[1 - c, j], FA + j)
        unpack_a(1 - c, j)
    for j in range(4):
        wait_recv(hb.at[1 - c, j], FB + j)
        unpack_b(1 - c, j)
    for zh in range(2):
        for h in range(2):
            for l in range(9):
                o_par[pl.ds(h * 288 + zh * 144, 144), pl.ds(l * 128, 128)] = o[zh, l, pl.ds(h * 144, 144), :].astype(BF16)

    for part in range(2):
        for cp in sib_copies(part):
            cp.wait_send()
    for d in range(1, 4):
        xt = (x + d) % 4
        wait_send(sa1.at[xt], A1 + xt)
        wait_send(ha.at[c, x], GA3 + xt)
    for j in range(4):
        @pl.when(4 * c + j != z)
        def _():
            wait_send(sb1.at[j], B1 + j)
            wait_send(sa2.at[j], A2 + j)

        wait_send(ha.at[c, j], FA + j)
        wait_send(hb.at[c, j], FB + j)

    @pl.when(act)
    def _():
        for d in range(1, 4):
            xt = (x + d) % 4
            wait_send(sb2.at[xt], B2 + xt)
            wait_send(gx.at[x], GB2 + xt)
        for d in range(1, 8):
            yt, zt = (y + d) % 8, (z + d) % 8
            wait_send(s3.at[yt // 4], Y3 + yt)
            wait_send(gz.at[z_lo], GA2 + zt)
            wait_send(hb.at[c, z_lo], GB3 + zt)
        wait_send(gs, SIB)
        wait_send(pb2.at[y_hi], G1)


def local(grad_parts, master, moment_one, moment_two, step_count):
    vm = pl.BlockSpec(memory_space=pltpu.VMEM)
    state = jax.ShapeDtypeStruct((9, D), F32)

    def vb(*shape):
        return pltpu.VMEM(shape, BF16)

    def vf(*shape):
        return pltpu.VMEM(shape, F32)

    return pl.pallas_call(
        kernel,
        out_shape=(state, state, state, state, jax.ShapeDtypeStruct((ROWS, D), BF16)),
        in_specs=[pl.BlockSpec(memory_space=pl.ANY), vm, vm, vm, pl.BlockSpec(memory_space=pltpu.SMEM)],
        out_specs=(vm, vm, vm, vm, vm),
        scratch_shapes=[
            vb(2, 144, D), vb(2, 144, D), vf(9, 288, 128),
            vb(4, 432, 128), vb(4, 432, 128), vb(4, 224, 128), vb(8, 224, 128),
            vf(448, 128), vf(256, 128), vf(224, 128),
            vb(4, 112, 128), vb(8, 112, 128), vb(4, 64, 128), vb(4, 64, 128),
            vb(2, 96, 128), vb(8, 96, 128),
            vf(96, 128), vf(96, 128), vb(2, 96, 128), vb(4, 112, 128), vb(4, 64, 128),
            vb(2, 4, 432, 128), vb(2, 4, 224, 128), vf(2, 9, 288, 128),
            pltpu.SemaphoreType.DMA((END,)), pltpu.SemaphoreType.DMA((END,)),
        ],
        compiler_params=pltpu.CompilerParams(collective_id=0, has_side_effects=True, vmem_limit_bytes=32 * 1024 * 1024),
        name="adam_step",
    )(grad_parts.reshape(ROWS, D), master, moment_one, moment_two, step_count)


def solution(mesh):
    owned = P("shard", None)
    return jax.shard_map(
        local,
        mesh=mesh,
        in_specs=(P("rep", "shard", None, None), owned, owned, owned, P()),
        out_specs=(owned, owned, owned, owned, P()),
        check_vma=False,
    )
```

time: 1020 us -> 62.8 us (0.06)
  waiting for transfers between devices: 928 us -> 0 us
  blocking collectives: 64.1 us -> 0 us
  Pallas kernels: 0 us -> 53.7 us
  between operations: 15.5 us -> 1.3 us
    unnamed x3 -> x0, waiting for transfers between devices: 797 us -> none
    all_gather x1 -> x0, waiting for transfers between devices: 131 us -> none  [local(): lax.all_gather(new_master.astype(jnp.bfloat16), 'shard', axis=0, tiled=True)]
    psum x1 -> x0, blocking collectives: 64.1 us -> none  [local(): summed = lax.psum(row_block, 'rep')]
    pallas_call x0 -> x1, Pallas kernels: none -> 53.7 us  [local(): pl.pallas_call(kernel, out_shape=(state, state, state, state, jax.ShapeDt...]
  transfers between devices with their start and end apart: 2 -> 0, of which waited for: 2 -> 0; matrix products, arithmetic and copies ran while one was open for 0% -> 0% of each run, Pallas kernels for 0% -> 0%
where the time goes in v1:
time: 62.8 us; the launch traced here: 62.5 us
  Pallas kernels  53.7 us (86%)
  local copies, waits for them, and re-layouts  7.56 us (12%)
  between operations  1.3 us (2%)
    pallas_call x1, Pallas kernels, local(): pl.pallas_call(kernel, out_shape=(state, state, state, state, jax.ShapeDt...  53.7 us
    unnamed x13, local copies, waits for them, and re-layouts  7.56 us

profile of v1, /device:TPU:1, one launch (start us, length us, event | category | flops | bytes accessed | tf_op | source)
XLA Modules:
  0.0 62.5 jit_solution(4576291268762545785)
XLA Ops:
  1.3 0.0 copy-start
  1.3 1.3 %copy-done = bf16[1,1,576,1152]{3,2,1,0:T(8,128)(2,1)S(1)} copy-done((bf16[1,1,576,1152]{3,2,1,0:T(8,128)(2,1)S(1)}, bf16[1,1,576,1152]{3,2,1,0:T(8,128)(2,1)}, u32[]{:S(2)}) %copy-start) | copy-done | bytes 1327128
  2.6 0.0 copy-start.1
  2.6 0.9 %copy-done.1 = f32[9,1152]{1,0:T(8,128)S(1)} copy-done((f32[9,1152]{1,0:T(8,128)S(1)}, f32[9,1152]{1,0:T(8,128)}, u32[]{:S(2)}) %copy-start.1) | copy-done | bytes 41496
  3.5 0.0 copy-start.2
  3.5 0.9 %copy-done.2 = f32[9,1152]{1,0:T(8,128)S(1)} copy-done((f32[9,1152]{1,0:T(8,128)S(1)}, f32[9,1152]{1,0:T(8,128)}, u32[]{:S(2)}) %copy-start.2) | copy-done | bytes 41496
  4.4 0.0 copy-start.3
  4.4 0.9 %copy-done.3 = f32[9,1152]{1,0:T(8,128)S(1)} copy-done((f32[9,1152]{1,0:T(8,128)S(1)}, f32[9,1152]{1,0:T(8,128)}, u32[]{:S(2)}) %copy-start.3) | copy-done | bytes 41496
  5.3 53.7 %adam_step.1 = (f32[9,1152]{1,0:T(8,128)S(1)}, f32[9,1152]{1,0:T(8,128)S(1)}, f32[9,1152]{1,0:T(8,128)S(1)}, f32[9,1152]{1,0:T(8,128)S(1)}, bf16[576,1152]{1,0:T(8,128)(2,1)S(1)}) custom-call(bf16[576,1152]{1,0:T(8,128)(2,1)S(1)} %bitcast.1, f32[9,1152]{1,0:T(8,128)S(1)} %copy-done.1, f32[9,1152]{1,0:T(8,128)S(1)} %copy-done.2, f32[9,1152]{1,0:T(8,128)S(1)} %copy-done.3, ...), custom_call_target="tpu_custom_call" | custom-call | tf_op jit(solution)/shard_map/adam_step/pallas_call | solution.py:344
  58.9 0.6 %copy.16 = f32[9,1152]{1,0:T(8,128)} copy(f32[9,1152]{1,0:T(8,128)S(1)} %get-tuple-element.10) | data formatting | bytes 82944
  59.6 0.6 %copy.17 = f32[9,1152]{1,0:T(8,128)} copy(f32[9,1152]{1,0:T(8,128)S(1)} %get-tuple-element.11) | data formatting | bytes 82944
  60.2 0.6 %copy.18 = f32[9,1152]{1,0:T(8,128)} copy(f32[9,1152]{1,0:T(8,128)S(1)} %get-tuple-element.12) | data formatting | bytes 82944
  60.8 0.6 %copy.19 = f32[9,1152]{1,0:T(8,128)} copy(f32[9,1152]{1,0:T(8,128)S(1)} %get-tuple-element.13) | data formatting | bytes 82944
  61.5 1.1 %copy.20 = bf16[576,1152]{1,0:T(8,128)(2,1)} copy(bf16[576,1152]{1,0:T(8,128)(2,1)S(1)} %get-tuple-element.14) | data formatting | bytes 2654208
Async XLA Ops:
  1.3 1.3 %copy-start = (bf16[1,1,576,1152]{3,2,1,0:T(8,128)(2,1)S(1)}, bf16[1,1,576,1152]{3,2,1,0:T(8,128)(2,1)}, u32[]{:S(2)}) copy-start(bf16[1,1,576,1152]{3,2,1,0:T(8,128)(2,1)} %param.5) | copy-start | bytes 3981316
  2.6 0.9 %copy-start.1 = (f32[9,1152]{1,0:T(8,128)S(1)}, f32[9,1152]{1,0:T(8,128)}, u32[]{:S(2)}) copy-start(f32[9,1152]{1,0:T(8,128)} %master.1) | copy-start | bytes 124420
  3.5 0.9 %copy-start.2 = (f32[9,1152]{1,0:T(8,128)S(1)}, f32[9,1152]{1,0:T(8,128)}, u32[]{:S(2)}) copy-start(f32[9,1152]{1,0:T(8,128)} %mom1.1) | copy-start | bytes 124420
  4.4 0.9 %copy-start.3 = (f32[9,1152]{1,0:T(8,128)S(1)}, f32[9,1152]{1,0:T(8,128)}, u32[]{:S(2)}) copy-start(f32[9,1152]{1,0:T(8,128)} %mom2.1) | copy-start | bytes 124420

commit v2 on v0

v2 whole, which is shorter than its diff:
```python
import math

import jax
import jax.numpy as jnp
from jax import lax
from jax.experimental import pallas as pl
from jax.experimental.pallas import tpu as pltpu
from jax.sharding import PartitionSpec as P

MESH = pl.DeviceIdType.MESH
F32, BF16 = jnp.float32, jnp.bfloat16
BETA_ONE = 0.9
BETA_TWO = 0.95
LEARN_RATE = 0.001
EPSILON = 1e-08

ROWS, D = 576, 1152
VMEM_BYTES = 48_000 * 1024
W = 384
CHUNKS = (2, 0, 1)


def fixes(step):
    steps = jnp.full((9, 128), step[0], jnp.int32).astype(F32)
    return 1.0 - jnp.exp(steps * math.log(BETA_ONE)), 1.0 - jnp.exp(steps * math.log(BETA_TWO))


def adam(total, master, mom1, mom2, first_fix, second_fix):
    g = total * (1.0 / 512.0)
    n1 = BETA_ONE * mom1 + (1.0 - BETA_ONE) * g
    n2 = BETA_TWO * mom2 + (1.0 - BETA_TWO) * g * g
    direction = n1 / first_fix / (jnp.sqrt(n2 / second_fix) + EPSILON)
    return master - LEARN_RATE * direction, n1, n2, direction


def finish(master, mom1, mom2, step, total, params, o_master, o_m1, o_m2, o_dir, o_par, new, sem):
    big = pltpu.make_async_copy(params, o_par, sem.at[3])
    big.start()
    first_fix, second_fix = fixes(step)
    for l in range(9):
        cols = pl.ds(l * 128, 128)
        made = adam(total[:, cols], master[:, cols], mom1[:, cols], mom2[:, cols], first_fix, second_fix)
        for i, v in enumerate(made):
            new[i, :, cols] = v
    outs = [pltpu.make_async_copy(new.at[i], ref, sem.at[4 + i]) for i, ref in enumerate((o_master, o_m1, o_m2, o_dir))]
    for cp in outs:
        cp.start()
    for cp in outs + [big]:
        cp.wait()


def kernel(
    grad, master, mom1, mom2, step,
    gn, out,
    state, own, sib, f, s1, ra1, rb1, acc, stage, s2, ra2, rb2, s3, r3, qs, gz, gx, ha, hb, o,
    send, recv, misc,
):
    rep, shard = lax.axis_index("rep"), lax.axis_index("shard")
    c, y_lo = rep % 2, rep // 2
    x, z, y_hi = shard % 4, (shard // 4) % 8, shard // 32
    y = y_hi * 4 + y_lo
    z_lo = z % 4
    act = z // 4 == c
    idle = jnp.logical_not(act)

    def dev(x_, y_, z_, c_):
        return ((y_ % 4) * 2 + c_, (y_ // 4) * 32 + z_ * 4 + x_)

    sibling = dev(x, y, z, 1 - c)

    barrier = pltpu.get_barrier_semaphore()

    def greet(where):
        pl.semaphore_signal(barrier, inc=1, device_id=where, device_id_type=MESH)

    for d in (4, 3, 5, 2, 6, 1, 7):
        greet(dev(x, y, (z + d) % 8, c))
        greet(dev(x, (y + d) % 8, z, c))
    for d in range(1, 4):
        greet(dev((x + d) % 4, y, z, c))
    greet(sibling)

    ends = {}

    def slot(name, i, n):
        if name not in ends:
            ends[name] = (sum(e[1] for e in ends.values()), n)
        return ends[name][0] + i

    started = []

    def rdma(src, dst, ssem, rsem, where):
        return pltpu.make_async_remote_copy(
            src_ref=src, dst_ref=dst, send_sem=send.at[ssem], recv_sem=recv.at[rsem], device_id=where, device_id_type=MESH
        )

    def push(src, dst, ssem, rsem, where, like, cond=None):
        rdma(src, dst, ssem, rsem, where).start()
        started.append((like, ssem, cond))

    def arrive(ref, rsem):
        rdma(ref, ref, rsem, rsem, sibling).wait_recv()

    def drain():
        for cond in (None, "act", 0, 1, 2, 3):
            mine = [e for e in started if e[2] == cond]
            if not mine:
                continue

            def waits(mine=mine):
                for like, ssem, _ in mine:
                    rdma(like(), like(), ssem, ssem, sibling).wait_send()

            if cond is None:
                waits()
            elif cond == "act":
                pl.when(act)(waits)
            else:
                pl.when(4 * c + cond != z)(waits)

    own_copies = {
        (ch, h): pltpu.make_async_copy(
            grad.at[pl.ds(pl.multiple_of(h * 288 + c * 144, 16), 144), pl.ds(ch * W, W)],
            own.at[h, :, pl.ds(ch * W, W)],
            misc.at[2 * ch + h],
        )
        for ch in CHUNKS
        for h in range(2)
    }
    state_copies = [pltpu.make_async_copy(ref, state.at[y_hi, i], misc.at[6 + i]) for i, ref in enumerate((master, mom1, mom2))]
    for cp in list(own_copies.values()) + state_copies:
        cp.start()
    pl.semaphore_wait(barrier, 18)

    for ch in CHUNKS:
        for h in range(2):
            to = sib.at[h, :, pl.ds(ch * W, W)]
            i = slot("s0", 2 * ch + h, 6)
            push(
                grad.at[pl.ds(pl.multiple_of(h * 288 + (1 - c) * 144, 16), 144), pl.ds(ch * W, W)],
                to, i, i, sibling, lambda to=to: to,
            )

    @pl.when(act)
    def _():
        for i, ref in enumerate((master, mom1, mom2)):
            k = slot("st", i, 3)
            push(ref, state.at[y_hi, i], k, k, dev(x, 7 - y, z, c), lambda: state.at[0, 0], "act")

    for ch in CHUNKS:
        acc[ch, pl.ds(216, 40), :] = jnp.zeros((40, 128), F32)
    stage[pl.ds(216, 8), :] = jnp.zeros((8, 128), F32)
    qs[...] = jnp.zeros((64, 128), F32)

    def add_pair(ch):
        for h in range(2):
            own_copies[ch, h].wait()
            arrive(sib.at[h, :, pl.ds(ch * W, W)], slot("s0", 2 * ch + h, 6))
            for l in range(3 * ch, 3 * ch + 3):
                cols = pl.ds(l * 128, 128)
                f[l, pl.ds(h * 144, 144), :] = own[h, :, cols].astype(F32) + sib[h, :, cols].astype(F32)

    add_pair(2)
    for j in range(4):
        for i in range(27):
            l, r = divmod(i, 9)
            for h in range(2):
                stage[pl.ds(i * 8 + h * 4, 4), :] = f[6 + l, pl.ds(h * 144 + j * 36 + r, 4, stride=9), :]
        s1[2, j] = stage[...].astype(BF16)
        zt = 4 * c + j

        @pl.when(zt != z)
        def _():
            push(s1.at[2, j], rb1.at[z], slot("b1", j, 8), slot("b1", z, 8), dev(x, y, zt, c), lambda: s1.at[2, 0], j)

    for ch in (0, 1):
        add_pair(ch)
        for d in (2, 1, 3, 0):
            xt = (x + d) % 4
            for i in range(27):
                l, r = divmod(i, 9)
                stage[pl.ds(8 * i, 8), :] = f[3 * ch + l, pl.ds(9 * xt + r, 8, stride=36), :]
            s1[ch, d] = stage[...].astype(BF16)
            if d:
                i = slot("a1", 4 * ch + d, 8)
                push(s1.at[ch, d], ra1.at[ch, d], i, i, dev(xt, y, z, c), lambda: s1.at[0, 0])
    def split(ch, t):
        return jnp.concatenate([acc[ch, pl.ds(h * 4 + t + 64 * i, 8, stride=8), :] for h in range(2) for i in range(4)], 0).astype(BF16)

    for ch in (0, 1):
        for d in range(1, 4):
            arrive(ra1.at[ch, d], slot("a1", 4 * ch + d, 8))
        total = s1[ch, 0].astype(F32)
        for d in range(1, 4):
            total += ra1[ch, d].astype(F32)
        acc[ch, pl.ds(0, 224), :] = total
        for j in range(4):
            zt = 4 * c + j
            s2[ch, j] = split(ch, j)

            @pl.when(zt != z)
            def _():
                push(s2.at[ch, j], ra2.at[ch, z], slot("a2", 4 * ch + j, 16), slot("a2", 8 * ch + z, 16), dev(x, y, zt, c), lambda: s2.at[0, 0], j)

    def to_y(ch, total):
        s3[ch] = total.astype(BF16)
        for d in (4, 3, 5, 2, 6, 1, 7):
            k = slot("y", 8 * ch + d, 24)
            push(s3.at[ch], r3.at[ch, d], k, k, dev(x, (y + d) % 8, z, c), lambda: s3.at[0], "act")

    def update(ch):
        for d in range(1, 8):
            arrive(r3.at[ch, d], slot("y", 8 * ch + d, 24))
        total = s3[ch].astype(F32)
        for d in range(1, 8):
            total += r3[ch, d].astype(F32)
        acc[ch, pl.ds(0, 64), :] = total
        for l in range(3):
            cols = pl.ds(ch * W + l * 128, 128)
            gn[:, cols] = acc[ch, pl.ds(pl.multiple_of(y_hi * 32, 32) + l * 9, 9), :]
            for h in range(2):
                qs[pl.ds(h * 32 + l * 9, 9), :] = adam(
                    acc[ch, pl.ds(h * 32 + l * 9, 9), :], state[h, 0, :, cols], state[h, 1, :, cols], state[h, 2, :, cols], *fixed
                )[0]
        return qs[...].astype(BF16)

    def z_gather(ch):
        gz[ch, z_lo] = update(ch)
        for d in (4, 3, 5, 2, 6, 1, 7):
            push(
                gz.at[ch, z_lo], gz.at[ch, z_lo], slot("ga2", 8 * ch + d, 16), slot("ga2", 8 * ch + z_lo, 16),
                dev(x, y, (z + d) % 8, c), lambda: gz.at[0, 0], "act",
            )

    def join(ch, blocks):
        for t in range(4):
            v = blocks[t].astype(F32)
            for h in range(2):
                for i in range(4):
                    acc[ch, pl.ds(h * 4 + t + 64 * i, 8, stride=8), :] = v[h * 32 + i * 8 : h * 32 + i * 8 + 8]
        return acc[ch, pl.ds(0, 224), :].astype(BF16)

    fixed = fixes(step)
    for cp in state_copies:
        cp.wait()

    @pl.when(act)
    def _():
        for d in range(1, 8):
            arrive(rb1.at[(z + d) % 8], slot("b1", (z + d) % 8, 8))
        total = s1[2, z_lo].astype(F32)
        for d in range(1, 8):
            total += rb1[(z + d) % 8].astype(F32)
        acc[2, pl.ds(0, 224), :] = total
        for d in (2, 1, 3, 0):
            xt = (x + d) % 4
            s2[2, d] = split(2, xt)
            if d:
                k = slot("b2", d, 4)
                push(s2.at[2, d], rb2.at[d], k, k, dev(xt, y, z, c), lambda: s2.at[0, 0], "act")

        for ch in (0, 2, 1):
            if ch == 2:
                for d in range(1, 4):
                    arrive(rb2.at[d], slot("b2", d, 4))
                total = s2[2, 0].astype(F32)
                for d in range(1, 4):
                    total += rb2[d].astype(F32)
            else:
                for d in range(1, 8):
                    arrive(ra2.at[ch, (z + d) % 8], slot("a2", 8 * ch + (z + d) % 8, 16))
                total = s2[ch, z_lo].astype(F32)
                for d in range(1, 8):
                    total += ra2[ch, (z + d) % 8].astype(F32)
            to_y(ch, total)

        for i in range(3):
            arrive(state.at[1 - y_hi, i], slot("st", i, 3))
        z_gather(0)
        gx[x] = update(2)
        for d in (2, 1, 3):
            push(gx.at[x], gx.at[x], slot("gb2", d, 4), slot("gb2", x, 4), dev((x + d) % 4, y, z, c), lambda: gx.at[0], "act")
        z_gather(1)
        k = slot("g", 0, 1)
        push(gn, gn, k, k, sibling, lambda: gn, "act")

        for d in range(1, 4):
            arrive(gx.at[(x + d) % 4], slot("gb2", (x + d) % 4, 4))
        hb[c, z_lo] = join(2, [gx[t] for t in range(4)])
        for d in (4, 3, 5, 2, 6, 1, 7):
            push(
                hb.at[c, z_lo], hb.at[c, z_lo], slot("gb3", d, 8), slot("gb3", z_lo, 8),
                dev(x, y, (z + d) % 8, c), lambda: hb.at[0, 0], "act",
            )

    for ch in (0, 1):
        for j in range(4):
            @pl.when(4 * c + j != z)
            def _():
                arrive(gz.at[ch, j], slot("ga2", 8 * ch + j, 16))

        ha[ch, c, x] = join(ch, [gz[ch, t] for t in range(4)])
        mine = ha.at[ch, c, x]
        for d in (2, 1, 3):
            push(mine, mine, slot("ga3", 4 * ch + d, 8), slot("ga3", 4 * ch + x, 8), dev((x + d) % 4, y, z, c), lambda: ha.at[0, 0, 0])
        push(mine, mine, slot("fa", 4 * ch, 8), slot("fa", 4 * ch + x, 8), sibling, lambda: ha.at[0, 0, 0])

    def unpack_a(ch, zh, xs):
        v = ha[ch, zh, xs].astype(F32)
        for i in range(27):
            l, r = divmod(i, 9)
            o[zh, 3 * ch + l, pl.ds(9 * xs + r, 8, stride=36), :] = v[8 * i : 8 * i + 8]

    def unpack_b(zh, j):
        v = hb[zh, j].astype(F32)
        for i in range(27):
            l, r = divmod(i, 9)
            for h in range(2):
                o[zh, 6 + l, pl.ds(h * 144 + j * 36 + r, 4, stride=9), :] = v[8 * i + 4 * h : 8 * i + 4 * h + 4]

    for ch in (0, 1):
        for d in (1, 3, 2):
            xs = (x + d) % 4
            ref = ha.at[ch, c, xs]
            arrive(ref, slot("ga3", 4 * ch + xs, 8))
            push(ref, ref, slot("fa", 4 * ch + d, 8), slot("fa", 4 * ch + xs, 8), sibling, lambda: ha.at[0, 0, 0])
        for t in range(4):
            unpack_a(ch, c, t)
    for j in range(4):
        @pl.when(4 * c + j != z)
        def _():
            arrive(hb.at[c, j], slot("gb3", j, 8))

        k = slot("fb", j, 4)
        push(hb.at[c, j], hb.at[c, j], k, k, sibling, lambda: hb.at[0, 0])
    for j in range(4):
        unpack_b(c, j)

    def write(ch):
        for l in range(3 * ch, 3 * ch + 3):
            for zh in range(2):
                for h in range(2):
                    out[pl.ds(h * 288 + zh * 144, 144), pl.ds(l * 128, 128)] = o[zh, l, pl.ds(h * 144, 144), :].astype(BF16)

    @pl.when(idle)
    def _():
        arrive(gn, slot("g", 0, 1))

    for ch in (0, 1):
        for t in range(4):
            arrive(ha.at[ch, 1 - c, t], slot("fa", 4 * ch + t, 8))
            unpack_a(ch, 1 - c, t)
        write(ch)
    for j in range(4):
        arrive(hb.at[1 - c, j], slot("fb", j, 4))
        unpack_b(1 - c, j)
    write(2)
    drain()


N_SEM = 160


def local(grad_parts, master, moment_one, moment_two, step_count):
    hbm = pl.BlockSpec(memory_space=pltpu.HBM)
    sm = pl.BlockSpec(memory_space=pltpu.SMEM)
    vm = pl.BlockSpec(memory_space=pltpu.VMEM)
    state = jax.ShapeDtypeStruct((9, D), F32)
    weights = jax.ShapeDtypeStruct((ROWS, D), BF16)

    def vb(*shape):
        return pltpu.VMEM(shape, BF16)

    def vf(*shape):
        return pltpu.VMEM(shape, F32)

    gradient = pltpu.with_memory_space_constraint(grad_parts.reshape(ROWS, D), pltpu.HBM)
    held = [pltpu.with_memory_space_constraint(a, pltpu.HBM) for a in (master, moment_one, moment_two)]
    summed, params = pl.pallas_call(
        kernel,
        out_shape=(state, weights),
        in_specs=[hbm, hbm, hbm, hbm, sm],
        out_specs=(vm, vm),
        scratch_shapes=[
            vf(2, 3, 9, D), vb(2, 144, D), vb(2, 144, D), vf(9, 288, 128),
            vb(3, 4, 224, 128), vb(2, 4, 224, 128), vb(8, 224, 128), vf(3, 256, 128), vf(224, 128),
            vb(3, 4, 64, 128), vb(2, 8, 64, 128), vb(4, 64, 128), vb(3, 64, 128), vb(3, 8, 64, 128),
            vf(64, 128), vb(2, 4, 64, 128), vb(4, 64, 128),
            vb(2, 2, 4, 224, 128), vb(2, 4, 224, 128), vf(2, 9, 288, 128),
            pltpu.SemaphoreType.DMA((N_SEM,)), pltpu.SemaphoreType.DMA((N_SEM,)), pltpu.SemaphoreType.DMA((13,)),
        ],
        compiler_params=pltpu.CompilerParams(collective_id=0, has_side_effects=True, vmem_limit_bytes=VMEM_BYTES),
        name="reduce_update_gather",
    )(gradient, *held, step_count)
    return pl.pallas_call(
        finish,
        out_shape=(state, state, state, state, weights),
        in_specs=[vm, vm, vm, sm, vm, vm],
        out_specs=(hbm,) * 5,
        scratch_shapes=[vf(4, 9, D), pltpu.SemaphoreType.DMA((8,))],
        compiler_params=pltpu.CompilerParams(vmem_limit_bytes=VMEM_BYTES),
        name="write_out",
    )(master, moment_one, moment_two, step_count, summed, params)


def solution(mesh):
    owned = P("shard", None)
    return jax.shard_map(
        local,
        mesh=mesh,
        in_specs=(P("rep", "shard", None, None), owned, owned, owned, P()),
        out_specs=(owned, owned, owned, owned, P()),
        check_vma=False,
    )
```

time: 1020 us -> 51.5 us (0.05)
  waiting for transfers between devices: 928 us -> 0 us
  blocking collectives: 64.1 us -> 0 us
  Pallas kernels: 0 us -> 50 us
  between operations: 15.5 us -> 1.37 us
    unnamed x3 -> x0, waiting for transfers between devices: 797 us -> none
    all_gather x1 -> x0, waiting for transfers between devices: 131 us -> none  [local(): lax.all_gather(new_master.astype(jnp.bfloat16), 'shard', axis=0, tiled=True)]
    psum x1 -> x0, blocking collectives: 64.1 us -> none  [local(): summed = lax.psum(row_block, 'rep')]
    pallas_call x0 -> x2, Pallas kernels: none -> 50 us  [the longest x1 48.7 us: local(): pl.pallas_call(kernel, out_shape=(state, weights), in_specs=[hbm, hbm, hb...]
  transfers between devices with their start and end apart: 2 -> 0, of which waited for: 2 -> 0; matrix products, arithmetic and copies ran while one was open for 0% -> 0% of each run, Pallas kernels for 0% -> 0%
where the time goes in v2:
time: 51.5 us; the launch traced here: 51.3 us
  Pallas kernels  50 us (97%)
  between operations  1.37 us (3%)
    pallas_call x1, Pallas kernels, local(): pl.pallas_call(kernel, out_shape=(state, weights), in_specs=[hbm, hbm, hb...  48.7 us
    pallas_call x1, Pallas kernels, local(): pl.pallas_call(finish, out_shape=(state, state, state, state, weights), i...  1.22 us

profile of v2, /device:TPU:1, one launch (start us, length us, event | category | flops | bytes accessed | tf_op | source)
XLA Modules:
  0.0 51.3 jit_solution(14154944063525819398)
XLA Ops:
  0.6 0.0 copy-start.2
  0.6 0.0 copy-start.1
  0.7 0.0 copy-start
  1.3 48.7 %reduce_update_gather.1 = (f32[9,1152]{1,0:T(8,128)S(1)}, bf16[576,1152]{1,0:T(8,128)(2,1)S(1)}) custom-call(bf16[576,1152]{1,0:T(8,128)(2,1)} %bitcast.1, f32[9,1152]{1,0:T(8,128)} %master.3, f32[9,1152]{1,0:T(8,128)} %mom1.3, f32[9,1152]{1,0:T(8,128)} %mom2.3, s32[1]{0:T(128)S(6)} %copy.10.step), custom_call_target="tpu_custom_call" | custom-call | tf_op jit(solution)/shard_map/reduce_update_gather/pallas_call | solution.py:379
  50.1 0.0 copy-done.2
  50.1 0.0 copy-done.1
  50.1 0.0 copy-done
  50.1 1.2 %write_out.1 = (f32[9,1152]{1,0:T(8,128)}, f32[9,1152]{1,0:T(8,128)}, f32[9,1152]{1,0:T(8,128)}, f32[9,1152]{1,0:T(8,128)}, bf16[576,1152]{1,0:T(8,128)(2,1)}) custom-call(f32[9,1152]{1,0:T(8,128)S(1)} %copy-done, f32[9,1152]{1,0:T(8,128)S(1)} %copy-done.1, f32[9,1152]{1,0:T(8,128)S(1)} %copy-done.2, s32[1]{0:T(128)S(6)} %copy.10.step, ...), custom_call_target="tpu_custom_call" | custom-call | tf_op jit(solution)/shard_map/write_out/pallas_call | solution.py:395
Async XLA Ops:
  0.6 49.5 %copy-start.2 = (f32[9,1152]{1,0:T(8,128)S(1)}, f32[9,1152]{1,0:T(8,128)}, u32[]{:S(2)}) copy-start(f32[9,1152]{1,0:T(8,128)} %mom2.3) | copy-start | bytes 124420
  0.6 49.5 %copy-start.1 = (f32[9,1152]{1,0:T(8,128)S(1)}, f32[9,1152]{1,0:T(8,128)}, u32[]{:S(2)}) copy-start(f32[9,1152]{1,0:T(8,128)} %mom1.3) | copy-start | bytes 124420
  0.7 49.5 %copy-start = (f32[9,1152]{1,0:T(8,128)S(1)}, f32[9,1152]{1,0:T(8,128)}, u32[]{:S(2)}) copy-start(f32[9,1152]{1,0:T(8,128)} %master.3) | copy-start | bytes 124420

commit v3 on v2

v3 whole, which is shorter than its diff:
```python
import math

import jax
import jax.numpy as jnp
from jax import lax
from jax.experimental import pallas as pl
from jax.experimental.pallas import tpu as pltpu
from jax.sharding import PartitionSpec as P

MESH = pl.DeviceIdType.MESH
F32, BF16 = jnp.float32, jnp.bfloat16
BETA_ONE = 0.9
BETA_TWO = 0.95
LEARN_RATE = 0.001
EPSILON = 1e-08

ROWS, D = 576, 1152
VMEM_BYTES = 48_000 * 1024
W = 384
CHUNKS = (2, 0, 1)


def fixes(step):
    steps = jnp.full((9, 128), step[0], jnp.int32).astype(F32)
    return 1.0 - jnp.exp(steps * math.log(BETA_ONE)), 1.0 - jnp.exp(steps * math.log(BETA_TWO))


def adam(total, master, mom1, mom2, first_fix, second_fix):
    g = total * (1.0 / 512.0)
    n1 = BETA_ONE * mom1 + (1.0 - BETA_ONE) * g
    n2 = BETA_TWO * mom2 + (1.0 - BETA_TWO) * g * g
    direction = n1 / first_fix / (jnp.sqrt(n2 / second_fix) + EPSILON)
    return master - LEARN_RATE * direction, n1, n2, direction


def finish(master, mom1, mom2, step, total, params, o_master, o_m1, o_m2, o_dir, o_par, new, sem):
    big = pltpu.make_async_copy(params, o_par, sem.at[3])
    big.start()
    first_fix, second_fix = fixes(step)
    for l in range(9):
        cols = pl.ds(l * 128, 128)
        made = adam(total[:, cols], master[:, cols], mom1[:, cols], mom2[:, cols], first_fix, second_fix)
        for i, v in enumerate(made):
            new[i, :, cols] = v
    outs = [pltpu.make_async_copy(new.at[i], ref, sem.at[4 + i]) for i, ref in enumerate((o_master, o_m1, o_m2, o_dir))]
    for cp in outs:
        cp.start()
    for cp in outs + [big]:
        cp.wait()


def kernel(
    grad, master, mom1, mom2, step,
    gn, out,
    state, own, sib, f, s1, ra1, rb1, acc, stage, s2, ra2, rb2, s3, r3, qs, gz, gx, ha, hb, o,
    send, recv, misc, here, ready,
):
    rep, shard = lax.axis_index("rep"), lax.axis_index("shard")
    c, y_lo = rep % 2, rep // 2
    x, z, y_hi = shard % 4, (shard // 4) % 8, shard // 32
    y = y_hi * 4 + y_lo
    z_lo = z % 4
    act = z // 4 == c
    idle = jnp.logical_not(act)

    def dev(x_, y_, z_, c_):
        return ((y_ % 4) * 2 + c_, (y_ // 4) * 32 + z_ * 4 + x_)

    sibling = dev(x, y, z, 1 - c)

    names = {}

    def sem(name, i=0):
        return names.setdefault((name, i), len(names))

    def rdma(src, dst, ssem, rsem, where):
        return pltpu.make_async_remote_copy(
            src_ref=src, dst_ref=dst, send_sem=send.at[ssem], recv_sem=recv.at[rsem], device_id=where, device_id_type=MESH
        )

    def push(src, dst, out_sem, in_sem, where):
        rdma(src, dst, out_sem, in_sem, where).start()

    def arrive(like, in_sem):
        rdma(like, like, 0, in_sem, sibling).wait_recv()

    def sent(like, out_sem):
        rdma(like, like, out_sem, 0, sibling).wait_send()

    barrier = pltpu.get_barrier_semaphore()

    def tell(sem_ref, where):
        pl.semaphore_signal(sem_ref, inc=1, device_id=where, device_id_type=MESH)

    def push_pair(ch):
        push(grad.at[:, 1 - c, :, pl.ds(ch * W, W)], sib.at[:, :, pl.ds(ch * W, W)], sem("s0"), sem("s0", ch), sibling)

    @pl.when(c == 1)
    def _():
        tell(barrier, sibling)

    @pl.when(c == 0)
    def _():
        pl.semaphore_wait(barrier, 1)
        tell(here, sibling)
        for d in (4, 3, 5, 2, 6, 1, 7):
            tell(barrier, dev(x, y, (z + d) % 8, 1))

    @pl.when(c == 1)
    def _():
        pl.semaphore_wait(here, 1)
        for d in (2, 1, 3):
            tell(barrier, dev((x + d) % 4, y, z, 1))
        for d in (4, 3, 5, 2, 6, 1, 7):
            tell(barrier, dev(x, (y + d) % 8, z, 1))

    def all_here():
        @pl.when(c == 1)
        def _():
            pl.semaphore_wait(barrier, 17)
            tell(ready, sibling)

        @pl.when(c == 0)
        def _():
            pl.semaphore_wait(ready, 1)

    for ch in CHUNKS:
        push_pair(ch)

    own_copies = [
        pltpu.make_async_copy(grad.at[:, c, :, pl.ds(ch * W, W)], own.at[:, :, pl.ds(ch * W, W)], misc.at[ch]) for ch in range(3)
    ]
    state_copies = [pltpu.make_async_copy(ref, state.at[y_hi, i], misc.at[3 + i]) for i, ref in enumerate((master, mom1, mom2))]
    for ch in CHUNKS:
        own_copies[ch].start()
    for cp in state_copies:
        cp.start()
    for ch in CHUNKS:
        acc[ch, pl.ds(216, 40), :] = jnp.zeros((40, 128), F32)
    stage[pl.ds(216, 8), :] = jnp.zeros((8, 128), F32)
    qs[...] = jnp.zeros((64, 128), F32)

    def add_pair(ch):
        own_copies[ch].wait()
        arrive(sib.at[:, :, pl.ds(ch * W, W)], sem("s0", ch))
        for h in range(2):
            for l in range(3 * ch, 3 * ch + 3):
                cols = pl.ds(l * 128, 128)
                f[l, pl.ds(h * 144, 144), :] = own[h, :, cols].astype(F32) + sib[h, :, cols].astype(F32)

    add_pair(2)
    for j in range(4):
        for i in range(27):
            l, r = divmod(i, 9)
            for h in range(2):
                stage[pl.ds(i * 8 + h * 4, 4), :] = f[6 + l, pl.ds(h * 144 + j * 36 + r, 4, stride=9), :]
        s1[2, j] = stage[...].astype(BF16)
        if j == 0:
            all_here()
        zt = 4 * c + j

        @pl.when(zt != z)
        def _():
            push(s1.at[2, j], rb1.at[z], sem("b1"), sem("b1"), dev(x, y, zt, c))

    for ch in (0, 1):
        add_pair(ch)
        for d in (2, 1, 3, 0):
            xt = (x + d) % 4
            for i in range(27):
                l, r = divmod(i, 9)
                stage[pl.ds(8 * i, 8), :] = f[3 * ch + l, pl.ds(9 * xt + r, 8, stride=36), :]
            s1[ch, d] = stage[...].astype(BF16)
            if d:
                push(s1.at[ch, d], ra1.at[ch, d - 1], sem("a1"), sem("a1", ch), dev(xt, y, z, c))
    @pl.when(act)
    def _():
        for i, ref in enumerate((master, mom1, mom2)):
            push(ref, state.at[y_hi, i], sem("st", i), sem("st", i), dev(x, 7 - y, z, c))

    def split(ch, t):
        return jnp.concatenate([acc[ch, pl.ds(h * 4 + t + 64 * i, 8, stride=8), :] for h in range(2) for i in range(4)], 0).astype(BF16)

    for ch in (0, 1):
        arrive(ra1.at[ch], sem("a1", ch))
        total = s1[ch, 0].astype(F32)
        for d in range(3):
            total += ra1[ch, d].astype(F32)
        acc[ch, pl.ds(0, 224), :] = total
        for j in range(4):
            zt = 4 * c + j
            s2[ch, j] = split(ch, j)

            @pl.when(zt != z)
            def _():
                push(s2.at[ch, j], ra2.at[ch, z], sem("a2"), sem("a2", ch), dev(x, y, zt, c))

    def to_y(ch, total):
        s3[ch] = total.astype(BF16)
        for d in (4, 3, 5, 2, 6, 1, 7):
            push(s3.at[ch], r3.at[ch, d - 1], sem("y"), sem("y", ch), dev(x, (y + d) % 8, z, c))

    def update(ch):
        arrive(r3.at[ch], sem("y", ch))
        total = s3[ch].astype(F32)
        for d in range(7):
            total += r3[ch, d].astype(F32)
        acc[ch, pl.ds(0, 64), :] = total
        for l in range(3):
            cols = pl.ds(ch * W + l * 128, 128)
            gn[:, cols] = acc[ch, pl.ds(pl.multiple_of(y_hi * 32, 32) + l * 9, 9), :]
            for h in range(2):
                qs[pl.ds(h * 32 + l * 9, 9), :] = adam(
                    acc[ch, pl.ds(h * 32 + l * 9, 9), :], state[h, 0, :, cols], state[h, 1, :, cols], state[h, 2, :, cols], *fixed
                )[0]
        return qs[...].astype(BF16)

    def z_gather(ch):
        gz[ch, z_lo] = update(ch)
        for d in (4, 3, 5, 2, 6, 1, 7):
            push(gz.at[ch, z_lo], gz.at[ch, z_lo], sem("ga2"), sem("ga2", ch), dev(x, y, (z + d) % 8, c))

    def join(ch, blocks):
        for t in range(4):
            v = blocks[t].astype(F32)
            for h in range(2):
                for i in range(4):
                    acc[ch, pl.ds(h * 4 + t + 64 * i, 8, stride=8), :] = v[h * 32 + i * 8 : h * 32 + i * 8 + 8]
        return acc[ch, pl.ds(0, 224), :].astype(BF16)

    fixed = fixes(step)
    for cp in state_copies:
        cp.wait()

    @pl.when(act)
    def _():
        arrive(rb1.at[pl.ds(0, 7)], sem("b1"))
        total = s1[2, z_lo].astype(F32)
        for d in range(1, 8):
            total += rb1[(z + d) % 8].astype(F32)
        acc[2, pl.ds(0, 224), :] = total
        for d in (2, 1, 3, 0):
            xt = (x + d) % 4
            s2[2, d] = split(2, xt)
            if d:
                push(s2.at[2, d], rb2.at[d - 1], sem("b2"), sem("b2"), dev(xt, y, z, c))

        for ch in (0, 2, 1):
            if ch == 2:
                arrive(rb2, sem("b2"))
                total = s2[2, 0].astype(F32)
                for d in range(3):
                    total += rb2[d].astype(F32)
            else:
                arrive(ra2.at[ch, pl.ds(0, 7)], sem("a2", ch))
                total = s2[ch, z_lo].astype(F32)
                for d in range(1, 8):
                    total += ra2[ch, (z + d) % 8].astype(F32)
            to_y(ch, total)

        for i in range(3):
            arrive(state.at[1 - y_hi, i], sem("st", i))
        z_gather(0)
        gx[x] = update(2)
        for d in (2, 1, 3):
            push(gx.at[x], gx.at[x], sem("gb2"), sem("gb2"), dev((x + d) % 4, y, z, c))
        z_gather(1)
        push(gn, gn, sem("g"), sem("g"), sibling)

        arrive(gx.at[pl.ds(0, 3)], sem("gb2"))
        hb[c, z_lo] = join(2, [gx[t] for t in range(4)])
        for d in (4, 3, 5, 2, 6, 1, 7):
            push(hb.at[c, z_lo], hb.at[c, z_lo], sem("gb3"), SEM_Z + z_lo, dev(x, y, (z + d) % 8, c))

    for ch in (0, 1):
        @pl.when(act)
        def _():
            arrive(gz.at[ch, pl.ds(0, 3)], sem("ga2", ch))

        @pl.when(idle)
        def _():
            arrive(gz.at[ch], sem("ga2", ch))

        ha[ch, c, x] = join(ch, [gz[ch, t] for t in range(4)])
        mine = ha.at[ch, c, x]
        for d in (2, 1, 3):
            push(mine, mine, sem("ga3"), SEM_X + 4 * ch + x, dev((x + d) % 4, y, z, c))
        push(mine, mine, sem("fa"), sem("fa", ch), sibling)

    def unpack_a(ch, zh, xs):
        v = ha[ch, zh, xs].astype(F32)
        for i in range(27):
            l, r = divmod(i, 9)
            o[zh, 3 * ch + l, pl.ds(9 * xs + r, 8, stride=36), :] = v[8 * i : 8 * i + 8]

    def unpack_b(zh, j):
        v = hb[zh, j].astype(F32)
        for i in range(27):
            l, r = divmod(i, 9)
            for h in range(2):
                o[zh, 6 + l, pl.ds(h * 144 + j * 36 + r, 4, stride=9), :] = v[8 * i + 4 * h : 8 * i + 4 * h + 4]

    for ch in (0, 1):
        for d in (1, 3, 2):
            xs = (x + d) % 4
            ref = ha.at[ch, c, xs]
            arrive(ref, SEM_X + 4 * ch + xs)
            push(ref, ref, sem("fa"), sem("fa", ch), sibling)
        for t in range(4):
            unpack_a(ch, c, t)
    for j in range(4):
        @pl.when(4 * c + j != z)
        def _():
            arrive(hb.at[c, j], SEM_Z + j)

        push(hb.at[c, j], hb.at[c, j], sem("fb"), sem("fb"), sibling)
    for j in range(4):
        unpack_b(c, j)

    def write(ch):
        for l in range(3 * ch, 3 * ch + 3):
            for zh in range(2):
                for h in range(2):
                    out[pl.ds(h * 288 + zh * 144, 144), pl.ds(l * 128, 128)] = o[zh, l, pl.ds(h * 144, 144), :].astype(BF16)

    @pl.when(idle)
    def _():
        arrive(gn, sem("g"))

    for ch in (0, 1):
        arrive(ha.at[ch, 1 - c], sem("fa", ch))
        for t in range(4):
            unpack_a(ch, 1 - c, t)
        write(ch)
    arrive(hb.at[1 - c], sem("fb"))
    for j in range(4):
        unpack_b(1 - c, j)
    write(2)

    sent(sib, sem("s0"))
    sent(ha.at[:, 0, pl.ds(0, 3)], sem("a1"))
    sent(ha.at[:, 0, pl.ds(0, 3)], sem("ga3"))
    sent(ha.at[:, 0], sem("fa"))
    sent(hb.at[0], sem("fb"))

    @pl.when(idle)
    def _():
        sent(s1.at[2], sem("b1"))
        sent(s2.at[pl.ds(0, 2)], sem("a2"))

    @pl.when(act)
    def _():
        sent(s1.at[2, pl.ds(0, 3)], sem("b1"))
        sent(s2.at[pl.ds(0, 2), pl.ds(0, 3)], sem("a2"))
        for i in range(3):
            sent(state.at[0, i], sem("st", i))
        sent(rb2, sem("b2"))
        sent(r3, sem("y"))
        sent(ra2.at[:, pl.ds(0, 7)], sem("ga2"))
        sent(rb2, sem("gb2"))
        sent(rb1.at[pl.ds(0, 7)], sem("gb3"))
        sent(gn, sem("g"))


N_SEM = 36
SEM_X, SEM_Z = 24, 32


def local(grad_parts, master, moment_one, moment_two, step_count):
    hbm = pl.BlockSpec(memory_space=pltpu.HBM)
    sm = pl.BlockSpec(memory_space=pltpu.SMEM)
    vm = pl.BlockSpec(memory_space=pltpu.VMEM)
    state = jax.ShapeDtypeStruct((9, D), F32)
    weights = jax.ShapeDtypeStruct((ROWS, D), BF16)

    def vb(*shape):
        return pltpu.VMEM(shape, BF16)

    def vf(*shape):
        return pltpu.VMEM(shape, F32)

    gradient = pltpu.with_memory_space_constraint(grad_parts.reshape(2, 2, 144, D), pltpu.HBM)
    held = [pltpu.with_memory_space_constraint(a, pltpu.HBM) for a in (master, moment_one, moment_two)]
    summed, params = pl.pallas_call(
        kernel,
        out_shape=(state, weights),
        in_specs=[hbm, hbm, hbm, hbm, sm],
        out_specs=(vm, vm),
        scratch_shapes=[
            vf(2, 3, 9, D), vb(2, 144, D), vb(2, 144, D), vf(9, 288, 128),
            vb(3, 4, 224, 128), vb(2, 3, 224, 128), vb(8, 224, 128), vf(3, 256, 128), vf(224, 128),
            vb(3, 4, 64, 128), vb(2, 8, 64, 128), vb(3, 64, 128), vb(3, 64, 128), vb(3, 7, 64, 128),
            vf(64, 128), vb(2, 4, 64, 128), vb(4, 64, 128),
            vb(2, 2, 4, 224, 128), vb(2, 4, 224, 128), vf(2, 9, 288, 128),
            pltpu.SemaphoreType.DMA((N_SEM,)), pltpu.SemaphoreType.DMA((N_SEM,)), pltpu.SemaphoreType.DMA((6,)),
            pltpu.SemaphoreType.REGULAR, pltpu.SemaphoreType.REGULAR,
        ],
        compiler_params=pltpu.CompilerParams(collective_id=0, has_side_effects=True, vmem_limit_bytes=VMEM_BYTES),
        name="reduce_update_gather",
    )(gradient, *held, step_count)
    return pl.pallas_call(
        finish,
        out_shape=(state, state, state, state, weights),
        in_specs=[vm, vm, vm, sm, vm, vm],
        out_specs=(hbm,) * 5,
        scratch_shapes=[vf(4, 9, D), pltpu.SemaphoreType.DMA((8,))],
        compiler_params=pltpu.CompilerParams(vmem_limit_bytes=VMEM_BYTES),
        name="write_out",
    )(master, moment_one, moment_two, step_count, summed, params)


def solution(mesh):
    owned = P("shard", None)
    return jax.shard_map(
        local,
        mesh=mesh,
        in_specs=(P("rep", "shard", None, None), owned, owned, owned, P()),
        out_specs=(owned, owned, owned, owned, P()),
        check_vma=False,
    )
```

time: 51.5 us -> 49 us (0.951)
  Pallas kernels: 50 us -> 47.5 us
    pallas_call x1, Pallas kernels: 48.7 us -> 46.2 us  [local(): pl.pallas_call(kernel, out_shape=(state, weights), in_specs=[hbm, hbm, hb...]
where the time goes in v3:
time: 49 us; the launch traced here: 48.9 us
  Pallas kernels  47.5 us (97%)
  between operations  1.37 us (3%)
    pallas_call x1, Pallas kernels, local(): pl.pallas_call(kernel, out_shape=(state, weights), in_specs=[hbm, hbm, hb...  46.2 us
    pallas_call x1, Pallas kernels, local(): pl.pallas_call(finish, out_shape=(state, state, state, state, weights), i...  1.22 us

profile of v3, /device:TPU:1, one launch (start us, length us, event | category | flops | bytes accessed | tf_op | source)
XLA Modules:
  0.0 48.9 jit_solution(18314237176699782504)
XLA Ops:
  0.6 0.0 copy-start.2
  0.6 0.0 copy-start.1
  0.7 0.0 copy-start
  1.3 46.2 %reduce_update_gather.1 = (f32[9,1152]{1,0:T(8,128)S(1)}, bf16[576,1152]{1,0:T(8,128)(2,1)S(1)}) custom-call(bf16[2,2,144,1152]{3,2,1,0:T(8,128)(2,1)} %bitcast.1, f32[9,1152]{1,0:T(8,128)} %master.3, f32[9,1152]{1,0:T(8,128)} %mom1.3, f32[9,1152]{1,0:T(8,128)} %mom2.3, s32[1]{0:T(128)S(6)} %copy.10.step), custom_call_target="tpu_custom_call" | custom-call | tf_op jit(solution)/shard_map/reduce_update_gather/pallas_call | solution.py:384
  47.6 0.0 copy-done.2
  47.6 0.0 copy-done.1
  47.6 0.0 copy-done
  47.6 1.2 %write_out.1 = (f32[9,1152]{1,0:T(8,128)}, f32[9,1152]{1,0:T(8,128)}, f32[9,1152]{1,0:T(8,128)}, f32[9,1152]{1,0:T(8,128)}, bf16[576,1152]{1,0:T(8,128)(2,1)}) custom-call(f32[9,1152]{1,0:T(8,128)S(1)} %copy-done, f32[9,1152]{1,0:T(8,128)S(1)} %copy-done.1, f32[9,1152]{1,0:T(8,128)S(1)} %copy-done.2, s32[1]{0:T(128)S(6)} %copy.10.step, ...), custom_call_target="tpu_custom_call" | custom-call | tf_op jit(solution)/shard_map/write_out/pallas_call | solution.py:401
Async XLA Ops:
  0.6 47.0 %copy-start.2 = (f32[9,1152]{1,0:T(8,128)S(1)}, f32[9,1152]{1,0:T(8,128)}, u32[]{:S(2)}) copy-start(f32[9,1152]{1,0:T(8,128)} %mom2.3) | copy-start | bytes 124420
  0.6 47.0 %copy-start.1 = (f32[9,1152]{1,0:T(8,128)S(1)}, f32[9,1152]{1,0:T(8,128)}, u32[]{:S(2)}) copy-start(f32[9,1152]{1,0:T(8,128)} %mom1.3) | copy-start | bytes 124420
  0.7 47.0 %copy-start = (f32[9,1152]{1,0:T(8,128)S(1)}, f32[9,1152]{1,0:T(8,128)}, u32[]{:S(2)}) copy-start(f32[9,1152]{1,0:T(8,128)} %master.3) | copy-start | bytes 124420

commit v4 on v3

v4 whole, which is shorter than its diff:
```python
import math

import jax
import jax.numpy as jnp
from jax import lax
from jax.experimental import pallas as pl
from jax.experimental.pallas import tpu as pltpu
from jax.sharding import PartitionSpec as P

MESH = pl.DeviceIdType.MESH
F32, BF16 = jnp.float32, jnp.bfloat16
BETA_ONE = 0.9
BETA_TWO = 0.95
LEARN_RATE = 0.001
EPSILON = 1e-08

ROWS, D = 576, 1152
VMEM_BYTES = 48_000 * 1024
CHUNKS = ((0, 3, "A"), (3, 2, "A"), (5, 2, "A"), (7, 2, "B"))
FIRST = (3, 0, 1, 2)
MIDDLE = (0, 3, 1, 2)
LAST = (0, 1, 2, 3)
IN_A = tuple(i for i, ch in enumerate(CHUNKS) if ch[2] == "A")
IN_B = tuple(i for i, ch in enumerate(CHUNKS) if ch[2] == "B")
GROUPS = tuple(n for _, n, _ in CHUNKS)
LONG = tuple(-(-72 * n // 16) * 16 for n in GROUPS)
HALF = tuple(-(-9 * n // 8) * 8 for n in GROUPS)
SHORT = tuple(2 * n for n in HALF)

SEM_LAST = 4 + 7 * len(CHUNKS)


def columns(ch):
    return pl.ds(CHUNKS[ch][0] * 128, CHUNKS[ch][1] * 128)


def scratch():
    found = {
        "state": ((2, 3, 9, D), F32), "own": ((2, 144, D), BF16), "sib": ((2, 144, D), BF16), "f": ((9, 288, 128), F32),
        "gn": None, "o": ((2, 9, 288, 128), F32),
    }
    for ch, (_, n, kind) in enumerate(CHUNKS):
        long, short = (LONG[ch], 128), (SHORT[ch], 128)
        found |= {
            f"acc{ch}": ((8 * HALF[ch] + 64, 128), F32), f"qs{ch}": (short, F32), f"stage{ch}": (long, F32),
            f"s1_{ch}": ((4,) + long, BF16), f"s2_{ch}": ((4,) + short, BF16), f"s3_{ch}": (short, BF16), f"r3_{ch}": ((7,) + short, BF16),
            f"r1_{ch}": ((3 if kind == "A" else 8,) + long, BF16), f"r2_{ch}": ((8 if kind == "A" else 3,) + short, BF16),
            f"g1_{ch}": ((4,) + short, BF16), f"g2_{ch}": ((2, 4) + long, BF16),
        }
    return {name: kind for name, kind in found.items() if kind}


def fixes(step):
    steps = jnp.full((9, 128), step[0], jnp.int32).astype(F32)
    return 1.0 - jnp.exp(steps * math.log(BETA_ONE)), 1.0 - jnp.exp(steps * math.log(BETA_TWO))


def adam(total, master, mom1, mom2, first_fix, second_fix):
    g = total * (1.0 / 512.0)
    n1 = BETA_ONE * mom1 + (1.0 - BETA_ONE) * g
    n2 = BETA_TWO * mom2 + (1.0 - BETA_TWO) * g * g
    direction = n1 / first_fix / (jnp.sqrt(n2 / second_fix) + EPSILON)
    return master - LEARN_RATE * direction, n1, n2, direction


def finish(master, mom1, mom2, step, total, params, o_master, o_m1, o_m2, o_dir, o_par, new, sem):
    big = pltpu.make_async_copy(params, o_par, sem.at[3])
    big.start()
    first_fix, second_fix = fixes(step)
    for l in range(9):
        cols = pl.ds(l * 128, 128)
        made = adam(total[:, cols], master[:, cols], mom1[:, cols], mom2[:, cols], first_fix, second_fix)
        for i, v in enumerate(made):
            new[i, :, cols] = v
    outs = [pltpu.make_async_copy(new.at[i], ref, sem.at[4 + i]) for i, ref in enumerate((o_master, o_m1, o_m2, o_dir))]
    for cp in outs:
        cp.start()
    for cp in outs + [big]:
        cp.wait()


def kernel(grad, master, mom1, mom2, step, gn, out, *refs):
    names = tuple(scratch())
    b = dict(zip(names, refs))
    send, recv, misc, here, ready = refs[len(names):]
    state, own, sib, f, o = (b[name] for name in ("state", "own", "sib", "f", "o"))

    def of(name):
        return [b[f"{name}{ch}"] for ch in range(len(CHUNKS))]

    acc, qs, stage = of("acc"), of("qs"), of("stage")
    s1, s2, s3, r1, r2, r3, g1, g2 = (of(name) for name in ("s1_", "s2_", "s3_", "r1_", "r2_", "r3_", "g1_", "g2_"))
    rep, shard = lax.axis_index("rep"), lax.axis_index("shard")
    c, y_lo = rep % 2, rep // 2
    x, z, y_hi = shard % 4, (shard // 4) % 8, shard // 32
    y = y_hi * 4 + y_lo
    z_lo = z % 4
    act = z // 4 == c
    idle = jnp.logical_not(act)

    def dev(x_, y_, z_, c_):
        return ((y_ % 4) * 2 + c_, (y_ // 4) * 32 + z_ * 4 + x_)

    sibling = dev(x, y, z, 1 - c)

    numbers = {}

    def sem(name, i=0):
        return numbers.setdefault((name, i), len(numbers))

    def rdma(src, dst, ssem, rsem, where):
        return pltpu.make_async_remote_copy(
            src_ref=src, dst_ref=dst, send_sem=send.at[ssem], recv_sem=recv.at[rsem], device_id=where, device_id_type=MESH
        )

    def push(src, dst, out_sem, in_sem, where):
        rdma(src, dst, out_sem, in_sem, where).start()

    def arrive(like, in_sem):
        rdma(like, like, 0, in_sem, sibling).wait_recv()

    def sent(like, out_sem):
        rdma(like, like, out_sem, 0, sibling).wait_send()

    barrier = pltpu.get_barrier_semaphore()

    def tell(sem_ref, where):
        pl.semaphore_signal(sem_ref, inc=1, device_id=where, device_id_type=MESH)

    def push_pair(ch):
        push(grad.at[:, 1 - c, :, columns(ch)], sib.at[:, :, columns(ch)], sem("s0"), sem("s0", ch), sibling)

    @pl.when(c == 1)
    def _():
        tell(barrier, sibling)

    @pl.when(c == 0)
    def _():
        pl.semaphore_wait(barrier, 1)
        tell(here, sibling)
        push_pair(FIRST[0])
        for d in (4, 3, 5, 2, 6, 1, 7):
            tell(barrier, dev(x, y, (z + d) % 8, 1))

    @pl.when(c == 1)
    def _():
        pl.semaphore_wait(here, 1)
        push_pair(FIRST[0])
        for d in (2, 1, 3):
            tell(barrier, dev((x + d) % 4, y, z, 1))
        for d in (4, 3, 5, 2, 6, 1, 7):
            tell(barrier, dev(x, (y + d) % 8, z, 1))

    def all_here():
        @pl.when(c == 1)
        def _():
            pl.semaphore_wait(barrier, 17)
            tell(ready, sibling)

        @pl.when(c == 0)
        def _():
            pl.semaphore_wait(ready, 1)

    for ch in FIRST[1:]:
        push_pair(ch)

    n_ch = len(CHUNKS)
    own_copies = [
        pltpu.make_async_copy(grad.at[:, c, :, columns(ch)], own.at[:, :, columns(ch)], misc.at[ch]) for ch in range(n_ch)
    ]
    state_copies = [pltpu.make_async_copy(ref, state.at[y_hi, i], misc.at[n_ch + i]) for i, ref in enumerate((master, mom1, mom2))]
    for ch in FIRST:
        own_copies[ch].start()
    for cp in state_copies:
        cp.start()
    for ch in range(n_ch):
        used = 72 * GROUPS[ch]
        acc[ch][pl.ds(used, acc[ch].shape[0] - used), :] = jnp.zeros((acc[ch].shape[0] - used, 128), F32)
        if LONG[ch] > used:
            stage[ch][pl.ds(used, LONG[ch] - used), :] = jnp.zeros((LONG[ch] - used, 128), F32)
        qs[ch][...] = jnp.zeros((SHORT[ch], 128), F32)

    def add_pair(ch):
        own_copies[ch].wait()
        arrive(sib.at[:, :, columns(ch)], sem("s0", ch))
        first, n, _ = CHUNKS[ch]
        for h in range(2):
            for l in range(first, first + n):
                cols = pl.ds(l * 128, 128)
                f[l, pl.ds(h * 144, 144), :] = own[h, :, cols].astype(F32) + sib[h, :, cols].astype(F32)

    for turn, ch in enumerate(FIRST):
        add_pair(ch)
        if turn == 0:
            all_here()
        first, n, kind = CHUNKS[ch]
        if kind == "B":
            for j in range(4):
                for i in range(9 * n):
                    l, r = divmod(i, 9)
                    for h in range(2):
                        stage[ch][pl.ds(i * 8 + h * 4, 4), :] = f[first + l, pl.ds(h * 144 + j * 36 + r, 4, stride=9), :]
                s1[ch][j] = stage[ch][...].astype(BF16)
                zt = 4 * c + j

                @pl.when(zt != z)
                def _():
                    push(s1[ch].at[j], r1[ch].at[z], sem("b1", ch), sem("b1", ch), dev(x, y, zt, c))
        else:
            for d in (2, 1, 3, 0):
                xt = (x + d) % 4
                for i in range(9 * n):
                    l, r = divmod(i, 9)
                    stage[ch][pl.ds(8 * i, 8), :] = f[first + l, pl.ds(9 * xt + r, 8, stride=36), :]
                s1[ch][d] = stage[ch][...].astype(BF16)
                if d:
                    push(s1[ch].at[d], r1[ch].at[d - 1], sem("a1", ch), sem("a1", ch), dev(xt, y, z, c))

    @pl.when(act)
    def _():
        for i, ref in enumerate((master, mom1, mom2)):
            push(ref, state.at[y_hi, i], sem("st", i), sem("st", i), dev(x, 7 - y, z, c))

    def split(ch, t):
        rows = [acc[ch][pl.ds(h * 4 + t + 64 * i, 8, stride=8), :] for h in range(2) for i in range(HALF[ch] // 8)]
        return jnp.concatenate(rows, 0).astype(BF16)

    def add_up(ch, mine, theirs, which):
        total = mine.astype(F32)
        for i in which:
            total += theirs[i].astype(F32)
        return total

    for ch in IN_A:
        arrive(r1[ch], sem("a1", ch))
        acc[ch][pl.ds(0, LONG[ch]), :] = add_up(ch, s1[ch][0], r1[ch], range(3))
        for j in range(4):
            zt = 4 * c + j
            s2[ch][j] = split(ch, j)

            @pl.when(zt != z)
            def _():
                push(s2[ch].at[j], r2[ch].at[z], sem("a2", ch), sem("a2", ch), dev(x, y, zt, c))

    def others_z():
        return [(z + d) % 8 for d in range(1, 8)]

    def to_y(ch, total):
        s3[ch][...] = total.astype(BF16)
        for d in (4, 3, 5, 2, 6, 1, 7):
            push(s3[ch], r3[ch].at[d - 1], sem("y", ch), sem("y", ch), dev(x, (y + d) % 8, z, c))

    def update(ch):
        arrive(r3[ch], sem("y", ch))
        acc[ch][pl.ds(0, SHORT[ch]), :] = add_up(ch, s3[ch][...], r3[ch], range(7))
        first, n, _ = CHUNKS[ch]
        half = HALF[ch]
        for l in range(n):
            cols = pl.ds((first + l) * 128, 128)
            gn[:, cols] = acc[ch][pl.ds(pl.multiple_of(y_hi * half, 8) + l * 9, 9), :]
            for h in range(2):
                qs[ch][pl.ds(h * half + l * 9, 9), :] = adam(
                    acc[ch][pl.ds(h * half + l * 9, 9), :], state[h, 0, :, cols], state[h, 1, :, cols], state[h, 2, :, cols], *fixed
                )[0]
        return qs[ch][...].astype(BF16)

    def join(ch):
        half = HALF[ch]
        for t in range(4):
            v = g1[ch][t].astype(F32)
            for h in range(2):
                for i in range(half // 8):
                    acc[ch][pl.ds(h * 4 + t + 64 * i, 8, stride=8), :] = v[h * half + i * 8 : h * half + i * 8 + 8]
        return acc[ch][pl.ds(0, LONG[ch]), :].astype(BF16)

    fixed = fixes(step)
    for cp in state_copies:
        cp.wait()

    @pl.when(act)
    def _():
        for ch in IN_B:
            arrive(r1[ch].at[pl.ds(0, 7)], sem("b1", ch))
            acc[ch][pl.ds(0, LONG[ch]), :] = add_up(ch, s1[ch][z_lo], r1[ch], others_z())
            for d in (2, 1, 3, 0):
                xt = (x + d) % 4
                s2[ch][d] = split(ch, xt)
                if d:
                    push(s2[ch].at[d], r2[ch].at[d - 1], sem("b2", ch), sem("b2", ch), dev(xt, y, z, c))

        for ch in MIDDLE:
            if ch in IN_B:
                arrive(r2[ch], sem("b2", ch))
                to_y(ch, add_up(ch, s2[ch][0], r2[ch], range(3)))
            else:
                arrive(r2[ch].at[pl.ds(0, 7)], sem("a2", ch))
                to_y(ch, add_up(ch, s2[ch][z_lo], r2[ch], others_z()))

        for i in range(3):
            arrive(state.at[1 - y_hi, i], sem("st", i))
        for ch in MIDDLE:
            if ch in IN_B:
                g1[ch][x] = update(ch)
                for d in (2, 1, 3):
                    push(g1[ch].at[x], g1[ch].at[x], sem("gb2", ch), sem("gb2", ch), dev((x + d) % 4, y, z, c))
            else:
                g1[ch][z_lo] = update(ch)
                for d in (4, 3, 5, 2, 6, 1, 7):
                    push(g1[ch].at[z_lo], g1[ch].at[z_lo], sem("ga2", ch), sem("ga2", ch), dev(x, y, (z + d) % 8, c))
        push(gn, gn, sem("g"), sem("g"), sibling)

        for k, ch in enumerate(IN_B):
            arrive(g1[ch].at[pl.ds(0, 3)], sem("gb2", ch))
            g2[ch][c, z_lo] = join(ch)
            for d in (4, 3, 5, 2, 6, 1, 7):
                push(g2[ch].at[c, z_lo], g2[ch].at[c, z_lo], sem("gb3", ch), SEM_LAST + 4 * ch + z_lo, dev(x, y, (z + d) % 8, c))

    for ch in IN_A:
        @pl.when(act)
        def _():
            arrive(g1[ch].at[pl.ds(0, 3)], sem("ga2", ch))

        @pl.when(idle)
        def _():
            arrive(g1[ch], sem("ga2", ch))

        g2[ch][c, x] = join(ch)
        mine = g2[ch].at[c, x]
        for d in (2, 1, 3):
            push(mine, mine, sem("ga3", ch), SEM_LAST + 4 * ch + x, dev((x + d) % 4, y, z, c))
        push(mine, mine, sem("f", ch), sem("f", ch), sibling)

    def unpack(ch, zh, t):
        first, n, kind = CHUNKS[ch]
        v = g2[ch][zh, t].astype(F32)
        for i in range(9 * n):
            l, r = divmod(i, 9)
            if kind == "A":
                o[zh, first + l, pl.ds(9 * t + r, 8, stride=36), :] = v[8 * i : 8 * i + 8]
            else:
                for h in range(2):
                    o[zh, first + l, pl.ds(h * 144 + t * 36 + r, 4, stride=9), :] = v[8 * i + 4 * h : 8 * i + 4 * h + 4]

    for ch in LAST:
        if ch in IN_A:
            for d in (1, 3, 2):
                xs = (x + d) % 4
                ref = g2[ch].at[c, xs]
                arrive(ref, SEM_LAST + 4 * ch + xs)
                push(ref, ref, sem("f", ch), sem("f", ch), sibling)
        else:
            for j in range(4):
                ref = g2[ch].at[c, j]

                @pl.when(4 * c + j != z)
                def _():
                    arrive(ref, SEM_LAST + 4 * ch + j)

                push(ref, ref, sem("f", ch), sem("f", ch), sibling)
        for t in range(4):
            unpack(ch, c, t)

    @pl.when(idle)
    def _():
        arrive(gn, sem("g"))

    for ch in LAST:
        arrive(g2[ch].at[1 - c], sem("f", ch))
        for t in range(4):
            unpack(ch, 1 - c, t)
        first, n, _ = CHUNKS[ch]
        for l in range(first, first + n):
            for zh in range(2):
                for h in range(2):
                    out[pl.ds(h * 288 + zh * 144, 144), pl.ds(l * 128, 128)] = o[zh, l, pl.ds(h * 144, 144), :].astype(BF16)

    sent(sib, sem("s0"))
    for ch in range(n_ch):
        sent(g2[ch].at[0], sem("f", ch))
    for ch in IN_A:
        sent(r1[ch], sem("a1", ch))
        sent(r1[ch], sem("ga3", ch))

    @pl.when(idle)
    def _():
        for ch in IN_A:
            sent(s2[ch], sem("a2", ch))
        for ch in IN_B:
            sent(s1[ch], sem("b1", ch))

    @pl.when(act)
    def _():
        for i in range(3):
            sent(state.at[0, i], sem("st", i))
        for ch in IN_A:
            sent(s2[ch].at[pl.ds(0, 3)], sem("a2", ch))
            sent(r3[ch], sem("ga2", ch))
        for ch in IN_B:
            sent(s1[ch].at[pl.ds(0, 3)], sem("b1", ch))
            sent(r2[ch], sem("b2", ch))
            sent(r2[ch], sem("gb2", ch))
            sent(r1[ch].at[pl.ds(0, 7)], sem("gb3", ch))
        for ch in range(n_ch):
            sent(r3[ch], sem("y", ch))
        sent(gn, sem("g"))

    if len(numbers) > SEM_LAST:
        raise ValueError(len(numbers))


N_SEM = SEM_LAST + 4 * len(CHUNKS)


def local(grad_parts, master, moment_one, moment_two, step_count):
    hbm = pl.BlockSpec(memory_space=pltpu.HBM)
    sm = pl.BlockSpec(memory_space=pltpu.SMEM)
    vm = pl.BlockSpec(memory_space=pltpu.VMEM)
    state = jax.ShapeDtypeStruct((9, D), F32)
    weights = jax.ShapeDtypeStruct((ROWS, D), BF16)

    def vf(*shape):
        return pltpu.VMEM(shape, F32)

    gradient = pltpu.with_memory_space_constraint(grad_parts.reshape(2, 2, 144, D), pltpu.HBM)
    held = [pltpu.with_memory_space_constraint(a, pltpu.HBM) for a in (master, moment_one, moment_two)]
    summed, params = pl.pallas_call(
        kernel,
        out_shape=(state, weights),
        in_specs=[hbm, hbm, hbm, hbm, sm],
        out_specs=(vm, vm),
        scratch_shapes=[
            *(pltpu.VMEM(*kind) for kind in scratch().values()),
            pltpu.SemaphoreType.DMA((SEM_LAST,)), pltpu.SemaphoreType.DMA((N_SEM,)), pltpu.SemaphoreType.DMA((3 + len(CHUNKS),)),
            pltpu.SemaphoreType.REGULAR, pltpu.SemaphoreType.REGULAR,
        ],
        compiler_params=pltpu.CompilerParams(collective_id=0, has_side_effects=True, vmem_limit_bytes=VMEM_BYTES),
        name="reduce_update_gather",
    )(gradient, *held, step_count)
    return pl.pallas_call(
        finish,
        out_shape=(state, state, state, state, weights),
        in_specs=[vm, vm, vm, sm, vm, vm],
        out_specs=(hbm,) * 5,
        scratch_shapes=[vf(4, 9, D), pltpu.SemaphoreType.DMA((8,))],
        compiler_params=pltpu.CompilerParams(vmem_limit_bytes=VMEM_BYTES),
        name="write_out",
    )(master, moment_one, moment_two, step_count, summed, params)


def solution(mesh):
    owned = P("shard", None)
    return jax.shard_map(
        local,
        mesh=mesh,
        in_specs=(P("rep", "shard", None, None), owned, owned, owned, P()),
        out_specs=(owned, owned, owned, owned, P()),
        check_vma=False,
    )
```

time: 49 us -> 48.1 us (0.982)
  Pallas kernels: 47.5 us -> 46.5 us
    pallas_call x1, Pallas kernels: 46.2 us -> 45.3 us  [local(): pl.pallas_call(kernel, out_shape=(state, weights), in_specs=[hbm, hbm, hb...]
where the time goes in v4:
time: 48.1 us; the launch traced here: 47.9 us
  Pallas kernels  46.5 us (97%)
  between operations  1.37 us (3%)
    pallas_call x1, Pallas kernels, local(): pl.pallas_call(kernel, out_shape=(state, weights), in_specs=[hbm, hbm, hb...  45.3 us
    pallas_call x1, Pallas kernels, local(): pl.pallas_call(finish, out_shape=(state, state, state, state, weights), i...  1.22 us

profile of v4, /device:TPU:1, one launch (start us, length us, event | category | flops | bytes accessed | tf_op | source)
XLA Modules:
  0.0 47.9 jit_solution(4564507684349834706)
XLA Ops:
  0.6 0.0 copy-start.2
  0.6 0.0 copy-start.1
  0.7 0.0 copy-start
  1.3 45.3 %reduce_update_gather.1 = (f32[9,1152]{1,0:T(8,128)S(1)}, bf16[576,1152]{1,0:T(8,128)(2,1)S(1)}) custom-call(bf16[2,2,144,1152]{3,2,1,0:T(8,128)(2,1)} %bitcast.1, f32[9,1152]{1,0:T(8,128)} %master.3, f32[9,1152]{1,0:T(8,128)} %mom1.3, f32[9,1152]{1,0:T(8,128)} %mom2.3, s32[1]{0:T(128)S(6)} %copy.10.step), custom_call_target="tpu_custom_call" | custom-call | tf_op jit(solution)/shard_map/reduce_update_gather/pallas_call | solution.py:426
  46.7 0.0 copy-done.2
  46.7 0.0 copy-done.1
  46.7 0.0 copy-done
  46.7 1.2 %write_out.1 = (f32[9,1152]{1,0:T(8,128)}, f32[9,1152]{1,0:T(8,128)}, f32[9,1152]{1,0:T(8,128)}, f32[9,1152]{1,0:T(8,128)}, bf16[576,1152]{1,0:T(8,128)(2,1)}) custom-call(f32[9,1152]{1,0:T(8,128)S(1)} %copy-done, f32[9,1152]{1,0:T(8,128)S(1)} %copy-done.1, f32[9,1152]{1,0:T(8,128)S(1)} %copy-done.2, s32[1]{0:T(128)S(6)} %copy.10.step, ...), custom_call_target="tpu_custom_call" | custom-call | tf_op jit(solution)/shard_map/write_out/pallas_call | solution.py:439
Async XLA Ops:
  0.6 46.0 %copy-start.2 = (f32[9,1152]{1,0:T(8,128)S(1)}, f32[9,1152]{1,0:T(8,128)}, u32[]{:S(2)}) copy-start(f32[9,1152]{1,0:T(8,128)} %mom2.3) | copy-start | bytes 124420
  0.6 46.0 %copy-start.1 = (f32[9,1152]{1,0:T(8,128)S(1)}, f32[9,1152]{1,0:T(8,128)}, u32[]{:S(2)}) copy-start(f32[9,1152]{1,0:T(8,128)} %mom1.3) | copy-start | bytes 124420
  0.7 46.0 %copy-start = (f32[9,1152]{1,0:T(8,128)S(1)}, f32[9,1152]{1,0:T(8,128)}, u32[]{:S(2)}) copy-start(f32[9,1152]{1,0:T(8,128)} %master.3) | copy-start | bytes 124420

commit v5 on v4

--- a/solution.py
+++ b/solution.py
@@ -19,7 +19,7 @@
 CHUNKS = ((0, 3, "A"), (3, 2, "A"), (5, 2, "A"), (7, 2, "B"))
 FIRST = (3, 0, 1, 2)
 MIDDLE = (0, 3, 1, 2)
-LAST = (0, 1, 2, 3)
+LAST = (0, 1, 3, 2)
 IN_A = tuple(i for i, ch in enumerate(CHUNKS) if ch[2] == "A")
 IN_B = tuple(i for i, ch in enumerate(CHUNKS) if ch[2] == "B")
 GROUPS = tuple(n for _, n, _ in CHUNKS)
@@ -91,17 +91,25 @@
     acc, qs, stage = of("acc"), of("qs"), of("stage")
     s1, s2, s3, r1, r2, r3, g1, g2 = (of(name) for name in ("s1_", "s2_", "s3_", "r1_", "r2_", "r3_", "g1_", "g2_"))
     rep, shard = lax.axis_index("rep"), lax.axis_index("shard")
-    c, y_lo = rep % 2, rep // 2
-    x, z, y_hi = shard % 4, (shard // 4) % 8, shard // 32
+    rem, div = lax.rem, lax.div
+    c, y_lo = rem(rep, 2), div(rep, 2)
+    x, z, y_hi = rem(shard, 4), rem(div(shard, 4), 8), div(shard, 32)
     y = y_hi * 4 + y_lo
-    z_lo = z % 4
-    act = z // 4 == c
+    z_lo = rem(z, 4)
+    act = div(z, 4) == c
     idle = jnp.logical_not(act)
 
-    def dev(x_, y_, z_, c_):
-        return ((y_ % 4) * 2 + c_, (y_ // 4) * 32 + z_ * 4 + x_)
-
-    sibling = dev(x, y, z, 1 - c)
+    sibling = (y_lo * 2 + 1 - c, shard)
+    xs_at = [rem(x + d, 4) for d in range(4)]
+    zs_at = [rem(z + d, 8) for d in range(8)]
+    ys_at = [rem(y + d, 8) for d in range(8)]
+    chips_x = [(y_lo, y_hi * 32 + z * 4 + i) for i in xs_at]
+    chips_z = [(y_lo, y_hi * 32 + i * 4 + x) for i in zs_at]
+    chips_y = [(rem(i, 4), div(i, 4) * 32 + z * 4 + x) for i in ys_at]
+    at_x, at_z, at_y = ([(i * 2 + c, j) for i, j in chips] for chips in (chips_x, chips_z, chips_y))
+    greet_x, greet_z, greet_y = ([(i * 2 + 1, j) for i, j in chips] for chips in (chips_x, chips_z, chips_y))
+    owners = [(rep, y_hi * 32 + (4 * c + j) * 4 + x) for j in range(4)]
+    mirror = ((3 - y_lo) * 2 + c, (1 - y_hi) * 32 + z * 4 + x)
 
     numbers = {}
 
@@ -140,16 +148,16 @@
         tell(here, sibling)
         push_pair(FIRST[0])
         for d in (4, 3, 5, 2, 6, 1, 7):
-            tell(barrier, dev(x, y, (z + d) % 8, 1))
+            tell(barrier, greet_z[d])
 
     @pl.when(c == 1)
     def _():
         pl.semaphore_wait(here, 1)
         push_pair(FIRST[0])
         for d in (2, 1, 3):
-            tell(barrier, dev((x + d) % 4, y, z, 1))
+            tell(barrier, greet_x[d])
         for d in (4, 3, 5, 2, 6, 1, 7):
-            tell(barrier, dev(x, (y + d) % 8, z, 1))
+            tell(barrier, greet_y[d])
 
     def all_here():
         @pl.when(c == 1)
@@ -205,21 +213,21 @@
 
                 @pl.when(zt != z)
                 def _():
-                    push(s1[ch].at[j], r1[ch].at[z], sem("b1", ch), sem("b1", ch), dev(x, y, zt, c))
+                    push(s1[ch].at[j], r1[ch].at[z], sem("b1", ch), sem("b1", ch), owners[j])
         else:
             for d in (2, 1, 3, 0):
-                xt = (x + d) % 4
+                xt = xs_at[d]
                 for i in range(9 * n):
                     l, r = divmod(i, 9)
                     stage[ch][pl.ds(8 * i, 8), :] = f[first + l, pl.ds(9 * xt + r, 8, stride=36), :]
                 s1[ch][d] = stage[ch][...].astype(BF16)
                 if d:
-                    push(s1[ch].at[d], r1[ch].at[d - 1], sem("a1", ch), sem("a1", ch), dev(xt, y, z, c))
+                    push(s1[ch].at[d], r1[ch].at[d - 1], sem("a1", ch), sem("a1", ch), at_x[d])
 
     @pl.when(act)
     def _():
         for i, ref in enumerate((master, mom1, mom2)):
-            push(ref, state.at[y_hi, i], sem("st", i), sem("st", i), dev(x, 7 - y, z, c))
+            push(ref, state.at[y_hi, i], sem("st", i), sem("st", i), mirror)
 
     def split(ch, t):
         rows = [acc[ch][pl.ds(h * 4 + t + 64 * i, 8, stride=8), :] for h in range(2) for i in range(HALF[ch] // 8)]
@@ -240,15 +248,15 @@
 
             @pl.when(zt != z)
             def _():
-                push(s2[ch].at[j], r2[ch].at[z], sem("a2", ch), sem("a2", ch), dev(x, y, zt, c))
+                push(s2[ch].at[j], r2[ch].at[z], sem("a2", ch), sem("a2", ch), owners[j])
 
     def others_z():
-        return [(z + d) % 8 for d in range(1, 8)]
+        return zs_at[1:]
 
     def to_y(ch, total):
         s3[ch][...] = total.astype(BF16)
         for d in (4, 3, 5, 2, 6, 1, 7):
-            push(s3[ch], r3[ch].at[d - 1], sem("y", ch), sem("y", ch), dev(x, (y + d) % 8, z, c))
+            push(s3[ch], r3[ch].at[d - 1], sem("y", ch), sem("y", ch), at_y[d])
 
     def update(ch):
         arrive(r3[ch], sem("y", ch))
@@ -283,10 +291,10 @@
             arrive(r1[ch].at[pl.ds(0, 7)], sem("b1", ch))
             acc[ch][pl.ds(0, LONG[ch]), :] = add_up(ch, s1[ch][z_lo], r1[ch], others_z())
             for d in (2, 1, 3, 0):
-                xt = (x + d) % 4
+                xt = xs_at[d]
                 s2[ch][d] = split(ch, xt)
                 if d:
-                    push(s2[ch].at[d], r2[ch].at[d - 1], sem("b2", ch), sem("b2", ch), dev(xt, y, z, c))
+                    push(s2[ch].at[d], r2[ch].at[d - 1], sem("b2", ch), sem("b2", ch), at_x[d])
 
         for ch in MIDDLE:
             if ch in IN_B:
@@ -302,18 +310,18 @@
             if ch in IN_B:
                 g1[ch][x] = update(ch)
                 for d in (2, 1, 3):
-                    push(g1[ch].at[x], g1[ch].at[x], sem("gb2", ch), sem("gb2", ch), dev((x + d) % 4, y, z, c))
+                    push(g1[ch].at[x], g1[ch].at[x], sem("gb2", ch), sem("gb2", ch), at_x[d])
             else:
                 g1[ch][z_lo] = update(ch)
                 for d in (4, 3, 5, 2, 6, 1, 7):
-                    push(g1[ch].at[z_lo], g1[ch].at[z_lo], sem("ga2", ch), sem("ga2", ch), dev(x, y, (z + d) % 8, c))
+                    push(g1[ch].at[z_lo], g1[ch].at[z_lo], sem("ga2", ch), sem("ga2", ch), at_z[d])
         push(gn, gn, sem("g"), sem("g"), sibling)
 
         for k, ch in enumerate(IN_B):
             arrive(g1[ch].at[pl.ds(0, 3)], sem("gb2", ch))
             g2[ch][c, z_lo] = join(ch)
             for d in (4, 3, 5, 2, 6, 1, 7):
-                push(g2[ch].at[c, z_lo], g2[ch].at[c, z_lo], sem("gb3", ch), SEM_LAST + 4 * ch + z_lo, dev(x, y, (z + d) % 8, c))
+                push(g2[ch].at[c, z_lo], g2[ch].at[c, z_lo], sem("gb3", ch), SEM_LAST + 4 * ch + z_lo, at_z[d])
 
     for ch in IN_A:
         @pl.when(act)
@@ -327,7 +335,7 @@
         g2[ch][c, x] = join(ch)
         mine = g2[ch].at[c, x]
         for d in (2, 1, 3):
-            push(mine, mine, sem("ga3", ch), SEM_LAST + 4 * ch + x, dev((x + d) % 4, y, z, c))
+            push(mine, mine, sem("ga3", ch), SEM_LAST + 4 * ch + x, at_x[d])
         push(mine, mine, sem("f", ch), sem("f", ch), sibling)
 
     def unpack(ch, zh, t):
@@ -344,7 +352,7 @@
     for ch in LAST:
         if ch in IN_A:
             for d in (1, 3, 2):
-                xs = (x + d) % 4
+                xs = xs_at[d]
                 ref = g2[ch].at[c, xs]
                 arrive(ref, SEM_LAST + 4 * ch + xs)
                 push(ref, ref, sem("f", ch), sem("f", ch), sibling)

time: 48.1 us -> 47.7 us (level)
  no operation moved by 1% of the time
where the time goes in v5:
time: 47.7 us; the launch traced here: 47.5 us
  Pallas kernels  46.2 us (97%)
  between operations  1.37 us (3%)
    pallas_call x1, Pallas kernels, local(): pl.pallas_call(kernel, out_shape=(state, weights), in_specs=[hbm, hbm, hb...  44.9 us
    pallas_call x1, Pallas kernels, local(): pl.pallas_call(finish, out_shape=(state, state, state, state, weights), i...  1.22 us

profile of v5, /device:TPU:1, one launch (start us, length us, event | category | flops | bytes accessed | tf_op | source)
XLA Modules:
  0.0 47.5 jit_solution(16538257008481177087)
XLA Ops:
  0.6 0.0 copy-start.2
  0.6 0.0 copy-start.1
  0.7 0.0 copy-start
  1.3 44.9 %reduce_update_gather.1 = (f32[9,1152]{1,0:T(8,128)S(1)}, bf16[576,1152]{1,0:T(8,128)(2,1)S(1)}) custom-call(bf16[2,2,144,1152]{3,2,1,0:T(8,128)(2,1)} %bitcast.1, f32[9,1152]{1,0:T(8,128)} %master.3, f32[9,1152]{1,0:T(8,128)} %mom1.3, f32[9,1152]{1,0:T(8,128)} %mom2.3, s32[1]{0:T(128)S(6)} %copy.10.step), custom_call_target="tpu_custom_call" | custom-call | tf_op jit(solution)/shard_map/reduce_update_gather/pallas_call | solution.py:434
  46.3 0.0 copy-done.2
  46.3 0.0 copy-done.1
  46.3 0.0 copy-done
  46.3 1.2 %write_out.1 = (f32[9,1152]{1,0:T(8,128)}, f32[9,1152]{1,0:T(8,128)}, f32[9,1152]{1,0:T(8,128)}, f32[9,1152]{1,0:T(8,128)}, bf16[576,1152]{1,0:T(8,128)(2,1)}) custom-call(f32[9,1152]{1,0:T(8,128)S(1)} %copy-done, f32[9,1152]{1,0:T(8,128)S(1)} %copy-done.1, f32[9,1152]{1,0:T(8,128)S(1)} %copy-done.2, s32[1]{0:T(128)S(6)} %copy.10.step, ...), custom_call_target="tpu_custom_call" | custom-call | tf_op jit(solution)/shard_map/write_out/pallas_call | solution.py:447
Async XLA Ops:
  0.6 45.7 %copy-start.2 = (f32[9,1152]{1,0:T(8,128)S(1)}, f32[9,1152]{1,0:T(8,128)}, u32[]{:S(2)}) copy-start(f32[9,1152]{1,0:T(8,128)} %mom2.3) | copy-start | bytes 124420
  0.6 45.7 %copy-start.1 = (f32[9,1152]{1,0:T(8,128)S(1)}, f32[9,1152]{1,0:T(8,128)}, u32[]{:S(2)}) copy-start(f32[9,1152]{1,0:T(8,128)} %mom1.3) | copy-start | bytes 124420
  0.7 45.7 %copy-start = (f32[9,1152]{1,0:T(8,128)S(1)}, f32[9,1152]{1,0:T(8,128)}, u32[]{:S(2)}) copy-start(f32[9,1152]{1,0:T(8,128)} %master.3) | copy-start | bytes 124420
